TPU v7x, 32 devices: a whole 2x2x4 slice. The times are simulated.
32 devices in a mesh: dp: 8 (over y, x, core), mp: 4 (over z).
Axes of the slice: x: 2, y: 2, z: 4, core: 2. Of those that a mesh axis runs over, the one named last changes fastest.
Arguments:
- inputs: bfloat16 [16, 1024, 768], P('dp', 'mp'), may hold values from -6 to 6
- lengths: int32 [16], P('dp'), may hold values from 100 to 1024, as said below
- ln1_gain: float32 [768], replicated, may hold values from 0.25 to 1.75
- ln1_bias: float32 [768], replicated, may hold values from -4 to 4
- w_qkv: bfloat16 [3, 768, 768], P(None, None, 'mp'), may hold values from -0.21875 to 0.21875
- b_qkv: float32 [3, 768], P(None, 'mp'), may hold values from -4 to 4
- w_out: bfloat16 [768, 768], P('mp'), may hold values from -1.75 to 1.75
- b_out: float32 [768], replicated, may hold values from -4 to 4
- ln2_gain: float32 [768], replicated, may hold values from 0.25 to 1.75
- ln2_bias: float32 [768], replicated, may hold values from -4 to 4
- w_up: bfloat16 [768, 3072], P(None, 'mp'), may hold values from -0.21875 to 0.21875
- b_up: bfloat16 [3072], P('mp'), may hold values from -4 to 4
- w_down: bfloat16 [3072, 768], P('mp'), may hold values from -0.109375 to 0.109375
- b_down: float32 [768], replicated, may hold values from -4 to 4
- cotangent: bfloat16 [16, 1024, 768], P('dp', 'mp'), may hold values from -12 to 12
Outputs:
- layer_out: bfloat16 [16, 1024, 768], P('dp', 'mp')
- grad_inputs: float32 [16, 1024, 768], P('dp', 'mp')
- grad_ln1_gain: float32 [768], replicated
- grad_ln1_bias: float32 [768], replicated
- grad_w_qkv: float32 [3, 768, 768], P(None, None, 'mp')
- grad_b_qkv: float32 [3, 768], P(None, 'mp')
- grad_w_out: float32 [768, 768], P('mp')
- grad_b_out: float32 [768], replicated
- grad_ln2_gain: float32 [768], replicated
- grad_ln2_bias: float32 [768], replicated
- grad_w_up: float32 [768, 3072], P(None, 'mp')
- grad_b_up: float32 [3072], P('mp')
- grad_w_down: float32 [3072, 768], P('mp')
- grad_b_down: float32 [768], replicated
Inputs may be any that keep to these rules, and one draw needn't show every extreme that they name: `lengths`: in each aligned block of 2 rows (the rows of one index of dp) one row, drawn from the seed, has all 1024 codons.
All inputs are finite; a program needn't handle non-finite values.
Results may differ from a plain program's by a relative error of at most 0.02.
Values may be sent and summed in bfloat16 or wider, within the bound.
A program may use at most 128 MiB of HBM per device.

v0:
```python
import math

import jax
import jax.numpy as jnp
from jax import lax
from jax.sharding import PartitionSpec as P

HDIM = 64


norm_eps = 1e-05
masked_score = -1000000000.0


def layer_norm(values, gain_vec, bias_vec):
    middle = jnp.mean(values, axis=-1, keepdims=True)
    centred = values - middle
    spread = jnp.mean(centred * centred, axis=-1, keepdims=True)
    return centred * lax.rsqrt(spread + norm_eps) * gain_vec + bias_vec


def rotary_tables(seq_len, head_size):
    freq_steps = jnp.arange(head_size // 2, dtype=jnp.float32)
    frequency = jnp.exp(freq_steps * (-2.0 * math.log(10000.0) / head_size))
    angles = jnp.arange(seq_len, dtype=jnp.float32)[:, None] * frequency[None, :]
    cosine = jnp.concatenate([jnp.cos(angles), jnp.cos(angles)], -1)
    sine_table = jnp.concatenate([jnp.sin(angles), jnp.sin(angles)], -1)
    return (cosine, sine_table)


def rotate(values, cosine, sine_table):
    half_size = values.shape[-1] // 2
    turned = jnp.concatenate([-values[..., half_size:], values[..., :half_size]], -1)
    return values * cosine[:, None, :] + turned * sine_table[:, None, :]


def rotate_back(grads_in, cosine, sine_table):
    half_size = grads_in.shape[-1] // 2
    scaled = grads_in * sine_table[:, None, :]
    turned = jnp.concatenate([scaled[..., half_size:], -scaled[..., :half_size]], -1)
    return grads_in * cosine[:, None, :] + turned


def gelu_slope(values):
    return (
        0.5 * (1.0 + lax.erf(values * 0.7071067811865476))
        + values * jnp.exp(-0.5 * values * values) * 0.3989422804014327
    )


def body(
    inputs,
    lengths,
    ln1_gain,
    ln1_bias,
    w_qkv,
    b_qkv,
    w_out,
    b_out,
    ln2_gain,
    ln2_bias,
    w_up,
    b_up,
    w_down,
    b_down,
    cotangent,
):
    row_count, local_len, model_width = inputs.shape
    full_len = local_len * lax.axis_size("mp")
    local_width = w_qkv.shape[2]
    head_size = HDIM
    heads_here = local_width // head_size
    offset = lax.axis_index("mp") * local_len
    local_pos = offset + jnp.arange(local_len, dtype=jnp.int32)
    local_keep = (local_pos[None, :] < lengths[:, None]).astype(jnp.float32)[:, :, None]
    key_keep = jnp.arange(full_len, dtype=jnp.int32)[None, :] < lengths[:, None]
    cosine, sine_table = rotary_tables(full_len, head_size)
    block_len = min(512, full_len)
    block_count = full_len // block_len
    att_scale = head_size ** (-0.5)
    x_float = inputs.astype(jnp.float32)
    normed_one = layer_norm(x_float, ln1_gain, ln1_bias).astype(jnp.bfloat16)
    piece_rows = lax.all_gather(normed_one, "mp", axis=1, tiled=True)
    qkv_raw = jnp.einsum("rld,tde->rlte", piece_rows, w_qkv, preferred_element_type=jnp.float32)
    normed_rows = piece_rows
    qkv_raw = qkv_raw + b_qkv[None, None]

    def split_heads(values):
        return values.reshape(row_count, full_len, heads_here, head_size)

    queries = rotate(split_heads(qkv_raw[:, :, 0]), cosine, sine_table).astype(jnp.bfloat16)
    key_rows = rotate(split_heads(qkv_raw[:, :, 1]), cosine, sine_table).astype(jnp.bfloat16)
    value_rows = split_heads(qkv_raw[:, :, 2]).astype(jnp.bfloat16)

    def by_blocks(values):
        return jnp.moveaxis(
            values.reshape(row_count, block_count, block_len, heads_here, head_size), 1, 0
        )

    def from_blocks(values):
        return jnp.moveaxis(values, 0, 1).reshape(row_count, full_len, heads_here, head_size)

    def scores_of(query_block):
        scores = (
            jnp.einsum("rqhe,rkhe->rhqk", query_block, key_rows, preferred_element_type=jnp.float32)
            * att_scale
        )
        return jnp.where(key_keep[:, None, None, :], scores, masked_score)

    def attend(query_block):
        scores = scores_of(query_block)
        row_max = jnp.max(scores, -1, keepdims=True)
        weights = jnp.exp(scores - row_max)
        row_total = jnp.sum(weights, -1, keepdims=True)
        weights_low = (weights / row_total).astype(jnp.bfloat16)
        mixed_block = jnp.einsum(
            "rhqk,rkhe->rqhe", weights_low, value_rows, preferred_element_type=jnp.float32
        )
        return (mixed_block.astype(jnp.bfloat16), row_max + jnp.log(row_total))

    mixed_blocks, log_totals = lax.map(attend, by_blocks(queries))
    mixed = from_blocks(mixed_blocks).reshape(row_count, full_len, local_width)
    attn_terms = jnp.einsum("rlc,cd->rld", mixed, w_out, preferred_element_type=jnp.float32)
    attn_local = (
        lax.psum_scatter(
            attn_terms.astype(jnp.bfloat16), "mp", scatter_dimension=1, tiled=True
        ).astype(jnp.float32)
        + b_out
    )
    residual = x_float + attn_local
    normed_two = layer_norm(residual, ln2_gain, ln2_bias).astype(jnp.bfloat16)
    grad_down = cotangent.astype(jnp.float32) * local_keep
    grad_down_low = grad_down.astype(jnp.bfloat16)
    grad_b_down = jnp.sum(grad_down, (0, 1))
    piece_rows = lax.all_gather(normed_two, "mp", axis=1, tiled=True)
    up_raw = jnp.einsum("rld,df->rlf", piece_rows, w_up, preferred_element_type=jnp.float32)
    normed_two_rows = piece_rows
    up_value = up_raw + b_up.astype(jnp.float32)
    activation = jax.nn.gelu(up_value, approximate=False).astype(jnp.bfloat16)
    down_terms = jnp.einsum("rlf,fd->rld", activation, w_down, preferred_element_type=jnp.float32)
    down_local = (
        lax.psum_scatter(
            down_terms.astype(jnp.bfloat16), "mp", scatter_dimension=1, tiled=True
        ).astype(jnp.float32)
        + b_down
    )
    layer_out = ((residual + down_local) * local_keep).astype(jnp.bfloat16)
    piece_rows = lax.all_gather(grad_down_low, "mp", axis=1, tiled=True)
    grad_act = jnp.einsum("rld,fd->rlf", piece_rows, w_down, preferred_element_type=jnp.float32)
    grad_down_rows = piece_rows
    grad_up = (grad_act * gelu_slope(up_value)).astype(jnp.bfloat16)
    grad_w_down = jnp.einsum(
        "rlf,rld->fd", activation, grad_down_rows, preferred_element_type=jnp.float32
    )
    grad_w_up = jnp.einsum(
        "rld,rlf->df", normed_two_rows, grad_up, preferred_element_type=jnp.float32
    )
    grad_b_up = jnp.sum(grad_up, (0, 1), dtype=jnp.float32)
    hidden_terms = jnp.einsum("rlf,df->rld", grad_up, w_up, preferred_element_type=jnp.float32)
    grad_normed_two = lax.psum_scatter(
        hidden_terms.astype(jnp.bfloat16), "mp", scatter_dimension=1, tiled=True
    ).astype(jnp.float32)
    unused_second, pull_second = jax.vjp(layer_norm, residual, ln2_gain, ln2_bias)
    grad_from_norm, grad_ln2_gain, grad_ln2_bias = pull_second(grad_normed_two)
    grad_residual = grad_down + grad_from_norm
    grad_attn = grad_residual.astype(jnp.bfloat16)
    grad_b_out = jnp.sum(grad_attn, (0, 1), dtype=jnp.float32)
    piece_rows = lax.all_gather(grad_attn, "mp", axis=1, tiled=True)
    grad_mixed_raw = jnp.einsum(
        "rld,cd->rlc", piece_rows, w_out, preferred_element_type=jnp.float32
    )
    grad_mixed = grad_mixed_raw.astype(jnp.bfloat16)
    grad_w_out = jnp.einsum("rlc,rld->cd", mixed, piece_rows, preferred_element_type=jnp.float32)

    def attend_back(carried, scan_item):
        grad_keys, grad_values = carried
        query_block, grad_block, log_total = scan_item
        probs_full = jnp.exp(scores_of(query_block) - log_total)
        grad_probs = jnp.einsum(
            "rqhe,rkhe->rhqk", grad_block, value_rows, preferred_element_type=jnp.float32
        )
        inner_sum = jnp.sum(probs_full * grad_probs, -1, keepdims=True)
        grad_scores = (probs_full * (grad_probs - inner_sum)).astype(jnp.bfloat16)
        grad_query = (
            jnp.einsum("rhqk,rkhe->rqhe", grad_scores, key_rows, preferred_element_type=jnp.float32)
            * att_scale
        )
        grad_keys = (
            grad_keys
            + jnp.einsum(
                "rhqk,rqhe->rkhe", grad_scores, query_block, preferred_element_type=jnp.float32
            )
            * att_scale
        )
        grad_values = grad_values + jnp.einsum(
            "rhqk,rqhe->rkhe",
            probs_full.astype(jnp.bfloat16),
            grad_block,
            preferred_element_type=jnp.float32,
        )
        return ((grad_keys, grad_values), grad_query)

    zero_heads = jnp.zeros((row_count, full_len, heads_here, head_size), jnp.float32)
    grad_mixed_heads = grad_mixed.reshape(row_count, full_len, heads_here, head_size)
    (grad_keys, grad_values), grad_query_blocks = lax.scan(
        attend_back,
        (zero_heads, zero_heads),
        (by_blocks(queries), by_blocks(grad_mixed_heads), log_totals),
    )
    grad_queries = from_blocks(grad_query_blocks)
    grad_qkv = jnp.stack(
        [
            rotate_back(grad_queries, cosine, sine_table),
            rotate_back(grad_keys, cosine, sine_table),
            grad_values,
        ],
        2,
    )
    grad_qkv = grad_qkv.reshape(row_count, full_len, 3, local_width).astype(jnp.bfloat16)
    grad_b_qkv = jnp.sum(grad_qkv, (0, 1), dtype=jnp.float32)
    grad_w_qkv = jnp.einsum(
        "rld,rlte->tde", normed_rows, grad_qkv, preferred_element_type=jnp.float32
    )
    first_terms = jnp.einsum("rlte,tde->rld", grad_qkv, w_qkv, preferred_element_type=jnp.float32)
    grad_normed_one = lax.psum_scatter(
        first_terms.astype(jnp.bfloat16), "mp", scatter_dimension=1, tiled=True
    ).astype(jnp.float32)
    unused_first, pull_first = jax.vjp(layer_norm, x_float, ln1_gain, ln1_bias)
    grad_from_first, grad_ln1_gain, grad_ln1_bias = pull_first(grad_normed_one)
    grad_inputs = grad_residual + grad_from_first
    grad_w_qkv, grad_b_qkv, grad_w_out, grad_w_up, grad_b_up, grad_w_down = lax.psum(
        (grad_w_qkv, grad_b_qkv, grad_w_out, grad_w_up, grad_b_up, grad_w_down), "dp"
    )
    grad_ln1_gain, grad_ln1_bias, grad_b_out, grad_ln2_gain, grad_ln2_bias, grad_b_down = lax.psum(
        (grad_ln1_gain, grad_ln1_bias, grad_b_out, grad_ln2_gain, grad_ln2_bias, grad_b_down),
        ("dp", "mp"),
    )
    return (
        layer_out,
        grad_inputs,
        grad_ln1_gain,
        grad_ln1_bias,
        grad_w_qkv,
        grad_b_qkv,
        grad_w_out,
        grad_b_out,
        grad_ln2_gain,
        grad_ln2_bias,
        grad_w_up,
        grad_b_up,
        grad_w_down,
        grad_b_down,
    )


def solution(mesh):
    return jax.shard_map(
        body,
        mesh=mesh,
        in_specs=(
            P("dp", "mp", None),
            P("dp"),
            P(),
            P(),
            P(None, None, "mp"),
            P(None, "mp"),
            P("mp", None),
            P(),
            P(),
            P(),
            P(None, "mp"),
            P("mp"),
            P("mp", None),
            P(),
            P("dp", "mp", None),
        ),
        out_specs=(
            P("dp", "mp", None),
            P("dp", "mp", None),
            P(),
            P(),
            P(None, None, "mp"),
            P(None, "mp"),
            P("mp", None),
            P(),
            P(),
            P(),
            P(None, "mp"),
            P("mp"),
            P("mp", None),
            P(),
        ),
        check_vma=False,
    )
```

profile of v0, /device:TPU:0, one launch (start us, length us, event | category | flops | bytes accessed | tf_op | source)
XLA Modules:
  0.0 799.0 jit_solution(15708029800011693861)
XLA Ops:
  11.4 2.4 fusion.70
  15.3 2.2 multiply_cosine_fusion
  18.4 61.7 %all-gather.5.cloned.1.call-done = bf16[2,1024,768]{2,1,0:T(8,128)(2,1)} async-done(((bf16[2,256,768]{2,1,0:T(8,128)(2,1)}), bf16[2,1024,768]{2,1,0:T(8,128)(2,1)}) %all-gather.5.cloned.1.call-update) | async-done | bytes 3145744 | tf_op jit(solution)/shard_map/all_gather | solution.py:83
  80.1 3.9 broadcast_add_fusion
  85.5 2.5 reshape_squeeze.9
  89.2 2.8 concatenate.39
  92.0 2.7 concatenate.40
  94.7 2.5 fusion.100
  98.7 21.2 %while.28 = (s32[]{:T(128)}, bf16[2,2,512,3,64]{2,4,3,1,0:T(8,128)(2,1)}, f32[2,2,3,512,1]{3,2,1,4,0:T(4,128)}, bf16[2,2,512,3,64]{2,4,3,1,0:T(8,128)(2,1)S(1)},...) while((s32[]{:T(128)}, ...), condition=%wide.region_5.6_spmd.clone, body=%wide.region_2.5_spmd.clone.sunk | while | flops 843250688 | bytes 46727392 | solution.py:121
  98.8 2.0 fusion.148
  100.8 3.1 fusion.149
  103.9 3.9 fusion.150
  109.4 2.0 fusion.148
  111.3 3.1 fusion.149
  114.5 3.9 fusion.150
  119.9 3.4 copy.36
  123.3 3.6 reshape_reshape.6
  126.8 3.9 convolution_convert_fusion
  130.8 59.0 %reduce-scatter.5.cloned.1.call-done = bf16[2,256,768]{2,1,0:T(8,128)(2,1)} async-done(((bf16[2,1024,768]{2,1,0:T(8,128)(2,1)}), bf16[2,256,768]{2,1,0:T(8,128)(2,1)}) %reduce-scatter.5.cloned.1.call-update) | async-done | bytes 786448 | tf_op jit(solution)/shard_map/reduce_scatter | solution.py:125
  194.2 2.0 add_convert_fusion.1
  196.9 2.2 fusion.82
  200.5 59.4 %all-gather.7.cloned.1.call-done = bf16[2,1024,768]{2,1,0:T(8,128)(2,1)} async-done(((bf16[2,256,768]{2,1,0:T(8,128)(2,1)}), bf16[2,1024,768]{2,1,0:T(8,128)(2,1)}) %all-gather.7.cloned.1.call-update) | async-done | bytes 3145744 | tf_op jit(solution)/shard_map/all_gather | solution.py:135
  259.9 10.3 %fusion.84 = (u8[1024,768]{1,0:T(8,128)(4,1)}, u8[1024,768]{1,0:T(8,128)(4,1)}, f32[2,1024,768]{2,1,0:T(8,128)}) fusion(f32[768]{0:T(1024)} %convert_element_type.108, bf16[2,1024,768]{2,1,0:T(8,128)(2,1)} %all-gather.7.cloned.1.call-done, bf16[768,768]{1,0:T(8,128)(2,1)S(1)} %copy-done), kind=kOutput, calls=%fused_computation.138 | convolution fusion | flops 2436366336 | bytes 12192768 | tf_op jit(solution)/shard_map/rld,df->rlf/dot_general | solution.py:136
  270.2 53.9 %all-gather.9.cloned.1.call-done = bf16[2,1024,768]{2,1,0:T(8,128)(2,1)} async-done(((bf16[2,256,768]{2,1,0:T(8,128)(2,1)}), bf16[2,1024,768]{2,1,0:T(8,128)(2,1)}) %all-gather.9.cloned.1.call-update) | async-done | bytes 3145744 | tf_op jit(solution)/shard_map/all_gather | solution.py:148
  324.0 7.5 convert_reduce_fusion
  331.6 1.7 copy-done.81
  333.2 4.0 convolution_convert_fusion.1
  337.3 59.0 %reduce-scatter.9.cloned.1.call-done = bf16[2,256,768]{2,1,0:T(8,128)(2,1)} async-done(((bf16[2,1024,768]{2,1,0:T(8,128)(2,1)}), bf16[2,256,768]{2,1,0:T(8,128)(2,1)}) %reduce-scatter.9.cloned.1.call-update) | async-done | bytes 786448 | tf_op jit(solution)/shard_map/reduce_scatter | solution.py:160
  396.4 2.5 convert_reduce_fusion.3
  400.5 3.5 convert_reduce_fusion.5
  404.1 63.6 %all-gather.11.cloned.1.call-done = bf16[2,1024,768]{2,1,0:T(8,128)(2,1)} async-done(((bf16[2,256,768]{2,1,0:T(8,128)(2,1)}), bf16[2,1024,768]{2,1,0:T(8,128)(2,1)}) %all-gather.11.cloned.1.call-update) | async-done | bytes 3145744 | tf_op jit(solution)/shard_map/all_gather | solution.py:168
  467.7 3.9 convolution_convert_fusion.3
  471.6 3.5 reshape_reshape.7
  475.1 2.1 copy.51
  477.2 45.4 %while.29 = (s32[]{:T(128)}, f32[2,1024,3,64]{1,3,2,0:T(8,128)S(1)}, f32[2,1024,3,64]{1,3,2,0:T(8,128)}, f32[2,2,512,3,64]{2,4,3,1,0:T(8,128)}, bf16[2,2,512,3,6...) while((s32[]{:T(128)}, ...), condition=%wide.region_15.16_spmd.clone, body=%wide.region_13.15_spmd.clone.sunk | while | flops 2062613504 | bytes 136946000 | solution.py:205
  477.3 1.8 fusion.160
  479.2 3.0 bitcast_add_fusion.5
  482.3 6.4 multiply_reduce_fusion.3
  488.6 6.6 multiply_convert_fusion.3
  496.7 2.0 fusion.161
  499.9 1.8 fusion.160
  501.8 3.0 bitcast_add_fusion.5
  504.9 6.3 multiply_reduce_fusion.3
  511.2 6.6 multiply_convert_fusion.3
  519.3 2.0 fusion.161
  522.6 2.5 convert.17
  527.9 2.4 copy.39
  530.3 3.4 reshape.246
  539.3 4.2 bitcast_convert_fusion
  544.6 16.1 %fusion.42 = bf16[2,1024,768]{2,1,0:T(8,128)(2,1)S(1)} fusion(f32[2,1024,768]{2,1,0:T(8,128)} %get-tuple-element.262, f32[768]{0:T(1024)S(1)} %copy-done.69, u8[1024,768]{1,0:T(8,128)(4,1)} %get-tuple-element.182, u8[1024,768]{1,0:T(8,128)(4,1)S(1)} %copy-done.35), kind=kLoop, calls=%fused_computation.52 | loop fusion | flops 111673344 | bytes 11013120 | tf_op jit(solution)/shard_map/convert_element_type | solution.py:139
  562.4 4.0 convolution_convert_fusion.2
  566.7 7.1 convolution_bitcast_fusion
  573.8 4.2 convolution_bitcast_fusion.1
  580.2 3.2 fusion.85
  583.6 2.1 convert_reduce_fusion.1
  585.7 15.2 %all-reduce.1 = (f32[3,192]{1,0:T(4,128)}, f32[768]{0:T(1024)}) all-reduce(f32[3,192]{1,0:T(4,128)S(1)} %convert_reduce_fusion.1, f32[768]{0:T(1024)S(1)} %copy-done.74), channel_id=1, replica_groups=mesh['dp'=8,'mp'=4] {'dp'}, use_global_device_ids=true, to_apply=%region_25.26 | all-reduce | flops 1344 | bytes 10752 | tf_op jit(solution)/shard_map/psum | solution.py:231
  601.0 1.7 reduce-scatter.11.cloned.1.call-done
  602.6 1.7 convert_reduce_fusion.2
  604.4 2.1 fusion.75
  606.5 58.8 %reduce-scatter.7.cloned.1.call-done = bf16[2,256,768]{2,1,0:T(8,128)(2,1)} async-done(((bf16[2,1024,768]{2,1,0:T(8,128)(2,1)}), bf16[2,256,768]{2,1,0:T(8,128)(2,1)}) %reduce-scatter.7.cloned.1.call-update) | async-done | bytes 786448 | tf_op jit(solution)/shard_map/reduce_scatter | solution.py:142
  665.3 3.9 add_add_fusion.2
  669.2 41.5 %all-reduce = (f32[768]{0:T(1024)}, f32[768]{0:T(1024)}, f32[768]{0:T(1024)}, f32[768]{0:T(1024)}, f32[768]{0:T(1024)}, /*index=5*/f32[768]{0:T(1024)}) all-reduce(f32[768]{0:T(1024)S(1)} %get-tuple-element.185, f32[768]{0:T(1024)S(1)} %get-tuple-element.189, f32[768]{0:T(1024)S(1)} %copy-done.72, ...), channel_id=1, replica_groups=mesh['dp'=8,'mp'=4] {'dp','mp'}, use_global_device_ids=true, to_apply=%region_20.21 | all-reduce | flops 4608 | bytes 36864 | tf_op jit(solution)/shard_map/psum | solution.py:234
  710.7 73.6 %all-reduce.5.cloned.1.call-done = (f32[3,768,192]{1,2,0:T(8,128)}, f32[192,768]{1,0:T(8,128)}, f32[768,768]{1,0:T(8,128)}, f32[768,768]{1,0:T(8,128)}) async-done(((f32[3,768,192]{1,2,0:T(8,128)}, f32[192,768]{1,0:T(8,128)}, f32[768,768]{1,0:T(8,128)}, f32[768,768]{1,0:T(8,128)}), (f32[3,768,192]{1,2,0:T(8,128)}, f32[192,768]{1,0:T(8,128)}, f32[768,768]{1,0:T(8,128)}, ...) | async-done | bytes 7077904 | tf_op jit(solution)/shard_map/psum | solution.py:231
  784.3 2.9 copy.80
  (257 shorter events, 45.7 us)
Async XLA Ops:
  7.2 252.7 %copy-start = (bf16[768,768]{1,0:T(8,128)(2,1)S(1)}, bf16[768,768]{1,0:T(8,128)(2,1)}, u32[]{:S(2)}) copy-start(bf16[768,768]{1,0:T(8,128)(2,1)} %param.29) | copy-start | bytes 3538948
  7.2 72.9 %all-gather.5.cloned.1.call-start = ((), (), s32[]{:S(2)}) async-start(), calls=%async_computation.4 | async-start | bytes 3932160 | tf_op jit(solution)/shard_map/all_gather | solution.py:83
  10.8 69.3 %copy-start.78 = (bf16[3,768,192]{1,2,0:T(8,128)(2,1)S(1)}, bf16[3,768,192]{1,2,0:T(8,128)(2,1)}, u32[]{:S(2)}) copy-start(bf16[3,768,192]{1,2,0:T(8,128)(2,1)} %param.23) | copy-start | bytes 2654212
  10.8 69.3 %copy-start.80 = (f32[3,192]{1,0:T(4,128)S(1)}, f32[3,192]{1,0:T(4,128)}, u32[]{:S(2)}) copy-start(f32[3,192]{1,0:T(4,128)} %param.24) | copy-start | bytes 6916
  13.8 176.1 %reduce-scatter.5.cloned.1.call-start = ((), (), s32[]{:S(2)}) async-start(), calls=%async_computation.5 | async-start | bytes 3932160 | tf_op jit(solution)/shard_map/reduce_scatter | solution.py:125
  89.2 5.5 copy-start.19
  100.8 3.1 copy-start.36
  103.9 3.9 copy-start.40
  111.3 3.1 copy-start.36
  114.5 3.9 copy-start.40
  119.9 6.9 copy-start.4
  119.9 10.9 %copy-start.8 = (bf16[2,1024,3,64]{1,3,2,0:T(8,128)(2,1)}, bf16[2,1024,3,64]{1,3,2,0:T(8,128)(2,1)S(1)}, u32[]{:S(2)}) copy-start(bf16[2,1024,3,64]{1,3,2,0:T(8,128)(2,1)S(1)} %get-tuple-element.474) | copy-start | bytes 2359300
  130.7 59.1 %copy-start.2 = (bf16[2,256,768]{2,1,0:T(8,128)(2,1)S(1)}, bf16[2,256,768]{2,1,0:T(8,128)(2,1)}, u32[]{:S(2)}) copy-start(bf16[2,256,768]{2,1,0:T(8,128)(2,1)} %param.19) | copy-start | bytes 2359300
  130.7 59.1 %copy-start.43 = (f32[768]{0:T(1024)S(1)}, f32[768]{0:T(1024)}, u32[]{:S(2)}) copy-start(f32[768]{0:T(1024)} %param.26) | copy-start | bytes 9220
  130.8 63.4 %copy-start.45 = (f32[768]{0:T(1024)S(1)}, f32[768]{0:T(1024)}, u32[]{:S(2)}) copy-start(f32[768]{0:T(1024)} %param.27) | copy-start | bytes 9220
  130.8 129.1 %all-gather.7.cloned.1.call-start = ((), (), s32[]{:S(2)}) async-start(), calls=%async_computation.6 | async-start | bytes 3932160 | tf_op jit(solution)/shard_map/all_gather | solution.py:135
  189.9 4.3 copy-start.6
  191.4 209.1 %copy-start.47 = (f32[2,256]{1,0:T(2,128)}, f32[2,256]{1,0:T(2,128)S(1)}, u32[]{:S(2)}) copy-start(f32[2,256]{1,0:T(2,128)S(1)} %broadcast_multiply_fusion.2) | copy-start | bytes 6148
  196.2 127.8 %all-gather.9.cloned.1.call-start = ((), (), s32[]{:S(2)}) async-start(), calls=%async_computation.8 | async-start | bytes 3932160 | tf_op jit(solution)/shard_map/all_gather | solution.py:148
  199.2 197.2 %reduce-scatter.9.cloned.1.call-start = ((), (), s32[]{:S(2)}) async-start(), calls=%async_computation.9 | async-start | bytes 3932160 | tf_op jit(solution)/shard_map/reduce_scatter | solution.py:160
  337.2 61.6 %copy-start.68 = (f32[2,256]{1,0:T(2,128)S(1)}, f32[2,256]{1,0:T(2,128)}, u32[]{:S(2)}) copy-start(f32[2,256]{1,0:T(2,128)} %copy-done.67) | copy-start | bytes 6148
  337.2 61.6 %copy-start.54 = (f32[2,256]{1,0:T(2,128)S(1)}, f32[2,256]{1,0:T(2,128)}, u32[]{:S(2)}) copy-start(f32[2,256]{1,0:T(2,128)} %copy-done.53) | copy-start | bytes 6148
  337.3 63.2 %copy-start.57 = (f32[2,256]{1,0:T(2,128)S(1)}, f32[2,256]{1,0:T(2,128)}, u32[]{:S(2)}) copy-start(f32[2,256]{1,0:T(2,128)} %copy-done.56) | copy-start | bytes 6148
  337.3 130.4 %all-gather.11.cloned.1.call-start = ((), (), s32[]{:S(2)}) async-start(), calls=%async_computation.10 | async-start | bytes 3932160 | tf_op jit(solution)/shard_map/all_gather | solution.py:168
  398.9 5.2 copy-start.59
  400.5 3.6 copy-start.63
  400.5 67.2 %copy-start.39 = (bf16[192,768]{1,0:T(8,128)(2,1)S(1)}, bf16[192,768]{1,0:T(8,128)(2,1)}, u32[]{:S(2)}) copy-start(bf16[192,768]{1,0:T(8,128)(2,1)} %param.25) | copy-start | bytes 884740
  404.1 198.6 %reduce-scatter.11.cloned.1.call-start = ((), (), s32[]{:S(2)}) async-start(), calls=%async_computation.11 | async-start | bytes 3932160 | tf_op jit(solution)/shard_map/reduce_scatter | solution.py:225
  471.6 5.6 copy-start.5
  471.6 5.6 copy-start.42
  479.2 3.1 copy-start.9
  482.3 6.4 copy-start.34
  501.8 3.1 copy-start.9
  504.9 6.4 copy-start.34
  536.6 43.0 %copy-start.24 = (bf16[2,1024,3,64]{1,3,2,0:T(8,128)(2,1)}, bf16[2,1024,3,64]{1,3,2,0:T(8,128)(2,1)S(1)}, u32[]{:S(2)}) copy-start(bf16[2,1024,3,64]{1,3,2,0:T(8,128)(2,1)S(1)} %fusion.80) | copy-start | bytes 2359300
  538.3 41.4 %copy-start.25 = (bf16[2,1024,1,192]{1,3,2,0:T(8,128)(2,1)}, bf16[2,1024,1,192]{1,3,2,0:T(8,128)(2,1)S(1)}, u32[]{:S(2)}) copy-start(bf16[2,1024,1,192]{1,3,2,0:T(8,128)(2,1)S(1)} %add_convert_fusion) | copy-start | bytes 2359300
  543.5 121.7 %reduce-scatter.7.cloned.1.call-start = ((), (), s32[]{:S(2)}) async-start(), calls=%async_computation.7 | async-start | bytes 3932160 | tf_op jit(solution)/shard_map/reduce_scatter | solution.py:142
  544.6 17.8 %copy-start.77 = (bf16[768,768]{1,0:T(8,128)(2,1)S(1)}, bf16[768,768]{1,0:T(8,128)(2,1)}, u32[]{:S(2)}) copy-start(bf16[768,768]{1,0:T(8,128)(2,1)} %param.31) | copy-start | bytes 3538948
  566.4 217.9 %all-reduce.5.cloned.1.call-start = ((), (), s32[]{:S(2)}) async-start(), calls=%async_computation.12 | async-start | bytes 14155776 | tf_op jit(solution)/shard_map/psum | solution.py:231
  566.7 7.1 copy-start.76
  566.7 7.1 copy-start.82
  573.8 4.2 copy-start.11
  573.8 4.2 copy-start.23
  583.4 19.2 %copy-start.50 = (f32[2,256]{1,0:T(2,128)S(1)}, f32[2,256]{1,0:T(2,128)}, u32[]{:S(2)}) copy-start(f32[2,256]{1,0:T(2,128)} %copy-done.49) | copy-start | bytes 6148
  583.4 19.2 %copy-start.51 = (f32[768]{0:T(1024)S(1)}, f32[768]{0:T(1024)}, u32[]{:S(2)}) copy-start(f32[768]{0:T(1024)} %param.21) | copy-start | bytes 9220
  583.4 19.2 %copy-start.3 = (bf16[2,256,768]{2,1,0:T(8,128)(2,1)S(1)}, bf16[2,256,768]{2,1,0:T(8,128)(2,1)}, u32[]{:S(2)}) copy-start(bf16[2,256,768]{2,1,0:T(8,128)(2,1)} %param.19) | copy-start | bytes 2359300
  583.4 20.9 %copy-start.66 = (f32[2,256]{1,0:T(2,128)S(1)}, f32[2,256]{1,0:T(2,128)}, u32[]{:S(2)}) copy-start(f32[2,256]{1,0:T(2,128)} %copy-done.65) | copy-start | bytes 6148
  583.5 20.9 %copy-start.62 = (f32[2,256]{1,0:T(2,128)S(1)}, f32[2,256]{1,0:T(2,128)}, u32[]{:S(2)}) copy-start(f32[2,256]{1,0:T(2,128)} %copy-done.61) | copy-start | bytes 6148
  583.5 81.8 %copy-start.7 = (bf16[2,256,768]{2,1,0:T(8,128)(2,1)S(1)}, bf16[2,256,768]{2,1,0:T(8,128)(2,1)}, u32[]{:S(2)}) copy-start(bf16[2,256,768]{2,1,0:T(8,128)(2,1)} %reduce-scatter.5.cloned.1.call-done) | copy-start | bytes 2359300
  583.5 81.8 %copy-start.13 = (bf16[2,256,768]{2,1,0:T(8,128)(2,1)S(1)}, bf16[2,256,768]{2,1,0:T(8,128)(2,1)}, u32[]{:S(2)}) copy-start(bf16[2,256,768]{2,1,0:T(8,128)(2,1)} %reduce-scatter.9.cloned.1.call-done) | copy-start | bytes 2359300
  583.5 81.8 %copy-start.15 = (bf16[2,256,768]{2,1,0:T(8,128)(2,1)S(1)}, bf16[2,256,768]{2,1,0:T(8,128)(2,1)}, u32[]{:S(2)}) copy-start(bf16[2,256,768]{2,1,0:T(8,128)(2,1)} %param.33) | copy-start | bytes 2359300
  583.5 81.8 %copy-start.44 = (f32[768]{0:T(1024)S(1)}, f32[768]{0:T(1024)}, u32[]{:S(2)}) copy-start(f32[768]{0:T(1024)} %param.26) | copy-start | bytes 9220
  583.5 81.8 %copy-start.46 = (f32[768]{0:T(1024)S(1)}, f32[768]{0:T(1024)}, u32[]{:S(2)}) copy-start(f32[768]{0:T(1024)} %param.27) | copy-start | bytes 9220
  583.5 81.7 %copy-start.48 = (f32[2,256]{1,0:T(2,128)S(1)}, f32[2,256]{1,0:T(2,128)}, u32[]{:S(2)}) copy-start(f32[2,256]{1,0:T(2,128)} %copy-done.47) | copy-start | bytes 6148
  583.5 81.7 %copy-start.55 = (f32[2,256]{1,0:T(2,128)S(1)}, f32[2,256]{1,0:T(2,128)}, u32[]{:S(2)}) copy-start(f32[2,256]{1,0:T(2,128)} %copy-done.53) | copy-start | bytes 6148
  583.5 81.7 %copy-start.58 = (f32[2,256]{1,0:T(2,128)S(1)}, f32[2,256]{1,0:T(2,128)}, u32[]{:S(2)}) copy-start(f32[2,256]{1,0:T(2,128)} %copy-done.56) | copy-start | bytes 6148
  583.6 81.7 %copy-start.60 = (f32[2,256]{1,0:T(2,128)S(1)}, f32[2,256]{1,0:T(2,128)}, u32[]{:S(2)}) copy-start(f32[2,256]{1,0:T(2,128)} %copy-done.59) | copy-start | bytes 6148
  583.6 81.7 %copy-start.64 = (f32[2,256]{1,0:T(2,128)S(1)}, f32[2,256]{1,0:T(2,128)}, u32[]{:S(2)}) copy-start(f32[2,256]{1,0:T(2,128)} %copy-done.63) | copy-start | bytes 6148
  583.6 81.7 %copy-start.73 = (f32[768]{0:T(1024)S(1)}, f32[768]{0:T(1024)}, u32[]{:S(2)}) copy-start(f32[768]{0:T(1024)} %param.32) | copy-start | bytes 9220
  606.5 62.8 %copy-start.70 = (f32[768]{0:T(1024)S(1)}, f32[768]{0:T(1024)}, u32[]{:S(2)}) copy-start(f32[768]{0:T(1024)} %get-tuple-element.187) | copy-start | bytes 9220
  606.5 62.8 %copy-start.71 = (f32[768]{0:T(1024)S(1)}, f32[768]{0:T(1024)}, u32[]{:S(2)}) copy-start(f32[768]{0:T(1024)} %get-tuple-element.183) | copy-start | bytes 9220
  606.5 62.7 %copy-start.72 = (f32[768]{0:T(1024)S(1)}, f32[768]{0:T(1024)}, u32[]{:S(2)}) copy-start(f32[768]{0:T(1024)} %get-tuple-element.237) | copy-start | bytes 9220
  784.3 3.8 copy-start.32
  788.1 3.9 copy-start.1
  (38 other events, 56.5 us)
Sparse Core Ops, SparseCore 0:
  13.9 66.1 all-gather.4
  130.9 58.9 reduce-scatter.4
  196.3 63.4 all-gather.6
  261.9 62.1 all-gather.8
  337.4 58.9 reduce-scatter.8
  404.2 63.4 all-gather.10
  543.7 58.9 reduce-scatter.10
  604.9 60.2 reduce-scatter.6
  670.1 114.1 all-reduce.4
where the time goes:
time: 809 us; the launch traced here: 799 us
  waiting for transfers between devices  491 us (61%)
  matrix products  98.9 us (12%)
  other arithmetic  83.9 us (10%)
  blocking collectives  56.7 us (7%)
  local copies, waits for them, and re-layouts  52.7 us (7%)
  between operations  15 us (2%)
    psum x1, waiting for transfers between devices, body(): lax.psum((grad_w_qkv, grad_b_qkv, grad_w_out, grad_w_up, grad_b_up, grad_...  73.6 us
    all_gather x1, waiting for transfers between devices, body(): piece_rows = lax.all_gather(grad_attn, 'mp', axis=1, tiled=True)  63.6 us
    all_gather x1, waiting for transfers between devices, body(): piece_rows = lax.all_gather(normed_one, 'mp', axis=1, tiled=True)  61.7 us
    all_gather x1, waiting for transfers between devices, body(): piece_rows = lax.all_gather(normed_two, 'mp', axis=1, tiled=True)  59.4 us
    reduce_scatter x1, waiting for transfers between devices, body(): lax.psum_scatter(attn_terms.astype(jnp.bfloat16), 'mp', scatter_dimension...  59 us
    reduce_scatter x1, waiting for transfers between devices, body(): lax.psum_scatter(hidden_terms.astype(jnp.bfloat16), 'mp', scatter_dimensi...  59 us
    reduce_scatter x1, waiting for transfers between devices, body(): lax.psum_scatter(down_terms.astype(jnp.bfloat16), 'mp', scatter_dimension...  58.8 us
    all_gather x1, waiting for transfers between devices, body(): piece_rows = lax.all_gather(grad_down_low, 'mp', axis=1, tiled=True)  53.9 us
  transfers between devices with their start and end apart: 9, of which 9 were waited for; matrix products, arithmetic and copies ran while one was open for 8% of the time, Pallas kernels for 0%

commit v1 on v0

v1 whole, which is shorter than its diff:
```python
import math

import jax
import jax.numpy as jnp
from jax import lax
from jax.sharding import PartitionSpec as P

HDIM = 64
norm_eps = 1e-05
masked_score = -1000000000.0
F32 = jnp.float32
BF16 = jnp.bfloat16


def rotary_tables(positions, head_size):
    freq_steps = jnp.arange(head_size // 2, dtype=F32)
    frequency = jnp.exp(freq_steps * (-2.0 * math.log(10000.0) / head_size))
    angles = positions.astype(F32)[:, None] * frequency[None, :]
    cosine = jnp.concatenate([jnp.cos(angles), jnp.cos(angles)], -1)
    sine_table = jnp.concatenate([jnp.sin(angles), jnp.sin(angles)], -1)
    return (cosine, sine_table)


def rotate(values, cosine, sine_table):
    half_size = values.shape[-1] // 2
    turned = jnp.concatenate([-values[..., half_size:], values[..., :half_size]], -1)
    return values * cosine[:, None, :] + turned * sine_table[:, None, :]


def rotate_back(grads_in, cosine, sine_table):
    half_size = grads_in.shape[-1] // 2
    scaled = grads_in * sine_table[:, None, :]
    turned = jnp.concatenate([scaled[..., half_size:], -scaled[..., :half_size]], -1)
    return grads_in * cosine[:, None, :] + turned


def gelu_slope(values):
    return (
        0.5 * (1.0 + lax.erf(values * 0.7071067811865476))
        + values * jnp.exp(-0.5 * values * values) * 0.3989422804014327
    )


def norm_stats(values):
    middle = jnp.mean(values, axis=-1, keepdims=True)
    centred = values - middle
    spread = jnp.mean(centred * centred, axis=-1, keepdims=True)
    scale = lax.rsqrt(spread + norm_eps)
    return centred * scale, scale


def norm_back(grad, unit, scale, gain):
    h = grad * gain
    return scale * (
        h
        - jnp.mean(h, axis=-1, keepdims=True)
        - unit * jnp.mean(h * unit, axis=-1, keepdims=True)
    )


class Links:
    def __init__(self):
        self.ndp = lax.axis_size("dp")
        self.nmp = lax.axis_size("mp")
        self.dp = lax.axis_index("dp")
        self.mp = lax.axis_index("mp")
        self.bits = self.ndp.bit_length() - 1
        self.low = min(3, self.bits)
        self.pieces = 1 << self.low

    def bit(self, b):
        return (self.dp >> b) & 1

    def pair(self, x, b):
        return lax.ppermute(x, "dp", [(i, i ^ (1 << b)) for i in range(self.ndp)])

    def across(self, x, j):
        return lax.ppermute(x, "mp", [(i, i ^ j) for i in range(self.nmp)])

    def row_perm(self, k, back):
        pairs = []
        for dp in range(self.ndp):
            for z in range(self.nmp):
                q, c = dp // 2, dp % 2
                src = dp * self.nmp + z
                dst = (2 * q + z // 2) * self.nmp + 2 * c + ((z % 2) ^ k)
                pairs.append((dst, src) if back else (src, dst))
        return pairs

    def to_rows(self, x):
        out = []
        for k in range(2):
            mine = lax.dynamic_index_in_dim(x, (self.mp % 2) ^ k, 0, keepdims=False)
            out.append(lax.ppermute(mine, ("dp", "mp"), self.row_perm(k, False)))
        return out

    def from_rows(self, blocks):
        got = [
            lax.ppermute(blocks[k], ("dp", "mp"), self.row_perm(k, True)) for k in range(2)
        ]
        odd = self.mp % 2 == 1
        return jnp.stack([jnp.where(odd, got[1], got[0]), jnp.where(odd, got[0], got[1])])

    def join(self, own, other, b, axis):
        return jnp.where(
            self.bit(b) == 1,
            jnp.concatenate([other, own], axis),
            jnp.concatenate([own, other], axis),
        )

    def orders(self):
        upper = list(range(1, self.low))
        return [upper, upper[::-1]]

    def gather_dp(self, piece):
        k, r, w = piece.shape
        halves = []
        for order, half in zip(self.orders(), (piece[:, : r // 2], piece[:, r // 2 :])):
            now = half.reshape((k,) + (1,) * self.low + (r // 2, w))
            for b in order + [0]:
                now = self.join(now, self.pair(now, b), b, 1 + self.low - 1 - b)
            halves.append(now)
        whole = jnp.concatenate(halves, axis=1 + self.low)
        return whole.reshape(k, self.pieces * r, w)

    def gather_weight(self, own):
        n, w = own.shape
        r = n // self.pieces
        mine = lax.dynamic_slice_in_dim(own, (self.dp % self.pieces) * r, r, 0)
        got = jnp.stack([self.across(mine, j) for j in range(1, self.nmp)])
        got = self.gather_dp(got)
        return self.by_mp([own] + [got[j] for j in range(self.nmp - 1)])

    def by_mp(self, items):
        stacked = jnp.stack(items)
        for b in range(self.nmp.bit_length() - 1):
            odd = ((self.mp >> b) & 1) == 1
            shape = stacked.shape
            high = self.nmp >> (b + 1)
            parts = stacked.reshape((high, 2, 1 << b) + shape[1:])
            stacked = jnp.where(odd, parts[:, ::-1], parts).reshape(shape)
        return stacked

    def scatter_dp(self, grad):
        m, n, w = grad.shape
        r = n // self.pieces
        parts = grad.astype(BF16).reshape((m,) + (2,) * self.low + (r, w))

        def halve(now, b):
            axis = 1 + self.low - 1 - b
            mine = self.bit(b)
            keep = lax.dynamic_slice_in_dim(now, mine, 1, axis)
            send = lax.dynamic_slice_in_dim(now, 1 - mine, 1, axis)
            got = self.pair(send, b)
            return (keep.astype(F32) + got.astype(F32)).astype(BF16)

        now = halve(parts, 0)
        halves = []
        rows_axis = 1 + self.low
        for order, part in zip(self.orders(), jnp.split(now, 2, axis=rows_axis)):
            for b in order:
                part = halve(part, b)
            halves.append(part.reshape(m, r // 2, w))
        return jnp.concatenate(halves, 1)

    def reduce_grad(self, grad):
        piece = self.scatter_dp(grad)
        total = lax.dynamic_index_in_dim(piece, self.mp, 0, keepdims=False).astype(F32)
        for j in range(1, self.nmp):
            send = lax.dynamic_index_in_dim(piece, self.mp ^ j, 0, keepdims=False)
            total = total + self.across(send, j).astype(F32)
        for b in range(self.low, self.bits):
            total = total + self.pair(total.astype(BF16), b).astype(F32)
        out = self.gather_dp(total.astype(BF16)[None])[0]
        return out.astype(F32)


def body(
    inputs,
    lengths,
    ln1_gain,
    ln1_bias,
    w_qkv,
    b_qkv,
    w_out,
    b_out,
    ln2_gain,
    ln2_bias,
    w_up,
    b_up,
    w_down,
    b_down,
    cotangent,
):
    net = Links()
    row_count, local_len, width = inputs.shape
    nmp = net.nmp
    heads = width // HDIM
    core = net.dp % 2
    z = net.mp
    other = net.pair(lengths, 0)
    four = jnp.where(core == 1, jnp.concatenate([other, lengths]), jnp.concatenate([lengths, other]))
    length = lax.dynamic_index_in_dim(four, z, 0, keepdims=False)

    def positions_of(c):
        blocks = [
            (2 * c + ((z % 2) ^ k)) * local_len + jnp.arange(local_len, dtype=jnp.int32)
            for k in range(2)
        ]
        return jnp.concatenate(blocks)

    pos_here = positions_of(core)
    pos_all = jnp.concatenate([pos_here, positions_of(1 - core)])
    keep = (pos_here < length).astype(F32)[:, None]
    key_keep = pos_all < length
    cosine, sine_table = rotary_tables(pos_here, HDIM)

    x_blocks = net.to_rows(inputs)
    lw = w_qkv.shape[2]
    w_qkv_t = jnp.swapaxes(w_qkv, 1, 2).reshape(3 * lw, width)
    wq_all = net.gather_weight(jnp.concatenate([w_qkv_t, w_out], 0))
    wq = wq_all[:, : 3 * lw].reshape(nmp, 3, lw, width)
    wo = wq_all[:, 3 * lw :].reshape(nmp * lw, width)
    small = jnp.concatenate([b_qkv.reshape(-1), b_up.astype(F32)])
    small_all = net.by_mp([small] + [net.across(small, j) for j in range(1, nmp)])
    bq_all = small_all[:, : 3 * lw].reshape(nmp, 3, lw)
    bu_all = small_all[:, 3 * lw :]
    wu = net.gather_weight(w_up)
    wd = net.gather_weight(w_down)
    g_blocks = net.to_rows(cotangent)

    x = jnp.concatenate(x_blocks).astype(F32)
    n_tok = x.shape[0]
    unit1, scale1 = norm_stats(x)
    normed_one = (unit1 * ln1_gain + ln1_bias).astype(BF16)
    qkv = jnp.einsum("ld,mted->ltme", normed_one, wq, preferred_element_type=F32)
    qkv = qkv + jnp.swapaxes(bq_all, 0, 1)[None]
    qkv = qkv.reshape(n_tok, 3, heads, HDIM)
    q = rotate(qkv[:, 0], cosine, sine_table).astype(BF16)
    k = rotate(qkv[:, 1], cosine, sine_table).astype(BF16)
    v = qkv[:, 2].astype(BF16)
    k_other = net.pair(k, 0)
    v_other = net.pair(v, 0)
    k_all = jnp.concatenate([k, k_other])
    v_all = jnp.concatenate([v, v_other])
    att_scale = HDIM ** (-0.5)
    scores = jnp.einsum("qhe,khe->hqk", q, k_all, preferred_element_type=F32) * att_scale
    scores = jnp.where(key_keep[None, None, :], scores, masked_score)
    row_max = jnp.max(scores, -1, keepdims=True)
    weights = jnp.exp(scores - row_max)
    probs = (weights / jnp.sum(weights, -1, keepdims=True)).astype(BF16)
    mixed = jnp.einsum("hqk,khe->qhe", probs, v_all, preferred_element_type=F32)
    mixed = mixed.astype(BF16).reshape(n_tok, width)
    residual = x + (jnp.dot(mixed, wo, preferred_element_type=F32) + b_out)
    unit2, scale2 = norm_stats(residual)
    normed_two = (unit2 * ln2_gain + ln2_bias).astype(BF16)
    up = jnp.einsum("ld,mdf->lmf", normed_two, wu, preferred_element_type=F32) + bu_all
    act = jax.nn.gelu(up, approximate=False).astype(BF16)
    down = jnp.einsum("lmf,mfd->ld", act, wd, preferred_element_type=F32) + b_down
    layer_rows = ((residual + down) * keep).astype(BF16)
    layer_out = net.from_rows([layer_rows[:local_len], layer_rows[local_len:]])

    grad_down = jnp.concatenate(g_blocks).astype(F32) * keep
    grad_down_low = grad_down.astype(BF16)
    grad_b_down = jnp.sum(grad_down, 0)
    grad_w_down = jnp.einsum("lmf,ld->mfd", act, grad_down_low, preferred_element_type=F32)
    grad_act = jnp.einsum("ld,mfd->lmf", grad_down_low, wd, preferred_element_type=F32)
    grad_up = (grad_act * gelu_slope(up)).astype(BF16)
    grad_b_up = jnp.sum(grad_up, 0, dtype=F32)
    grad_w_up = jnp.einsum("ld,lmf->mdf", normed_two, grad_up, preferred_element_type=F32)
    grad_normed_two = jnp.einsum("lmf,mdf->ld", grad_up, wu, preferred_element_type=F32)
    grad_ln2_gain = jnp.sum(grad_normed_two * unit2, 0)
    grad_ln2_bias = jnp.sum(grad_normed_two, 0)
    grad_residual = grad_down + norm_back(grad_normed_two, unit2, scale2, ln2_gain)
    grad_w_down = net.reduce_grad(grad_w_down)
    grad_w_up = net.reduce_grad(grad_w_up)

    grad_attn = grad_residual.astype(BF16)
    grad_b_out = jnp.sum(grad_attn, 0, dtype=F32)
    grad_w_out = jnp.dot(mixed.T, grad_attn, preferred_element_type=F32)
    grad_mixed = jnp.einsum("ld,cd->lc", grad_attn, wo, preferred_element_type=F32).astype(BF16)
    inner_sum = jnp.sum(
        (grad_mixed.astype(F32) * mixed.astype(F32)).reshape(n_tok, heads, HDIM), -1
    )
    grad_mixed = grad_mixed.reshape(n_tok, heads, HDIM)
    grad_probs = jnp.einsum("qhe,khe->hqk", grad_mixed, v_all, preferred_element_type=F32)
    grad_scores = (probs.astype(F32) * (grad_probs - inner_sum.T[:, :, None])).astype(BF16)
    grad_v = jnp.einsum("hqk,qhe->khe", probs, grad_mixed, preferred_element_type=F32)
    grad_q = jnp.einsum("hqk,khe->qhe", grad_scores, k_all, preferred_element_type=F32) * att_scale
    grad_k = jnp.einsum("hqk,qhe->khe", grad_scores, q, preferred_element_type=F32) * att_scale
    grad_k = grad_k[:n_tok] + net.pair(grad_k[n_tok:].astype(BF16), 0).astype(F32)
    grad_v = grad_v[:n_tok] + net.pair(grad_v[n_tok:].astype(BF16), 0).astype(F32)
    grad_qkv = jnp.stack(
        [
            rotate_back(grad_q, cosine, sine_table),
            rotate_back(grad_k, cosine, sine_table),
            grad_v,
        ],
        1,
    )
    grad_qkv = grad_qkv.astype(BF16).reshape(n_tok, 3, nmp, lw)
    grad_b_qkv = jnp.sum(grad_qkv, 0, dtype=F32)
    grad_w_qkv = jnp.einsum("ltme,ld->mted", grad_qkv, normed_one, preferred_element_type=F32)
    first = jnp.einsum("ltme,mted->ld", grad_qkv, wq, preferred_element_type=F32)
    grad_ln1_gain = jnp.sum(first * unit1, 0)
    grad_ln1_bias = jnp.sum(first, 0)
    grad_x = (grad_residual + norm_back(first, unit1, scale1, ln1_gain)).astype(BF16)
    grad_inputs = net.from_rows([grad_x[:local_len], grad_x[local_len:]]).astype(F32)
    packed = net.reduce_grad(
        jnp.concatenate(
            [grad_w_qkv.reshape(nmp, 3 * lw, width), grad_w_out.reshape(nmp, lw, width)], 1
        )
    )
    grad_w_qkv = jnp.swapaxes(packed[: 3 * lw].reshape(3, lw, width), 1, 2)
    grad_w_out = packed[3 * lw :]

    vec = jnp.concatenate(
        [
            grad_ln1_gain,
            grad_ln1_bias,
            grad_b_out,
            grad_ln2_gain,
            grad_ln2_bias,
            grad_b_down,
            jnp.swapaxes(grad_b_qkv, 0, 1).reshape(-1),
            grad_b_up.reshape(-1),
        ]
    )
    vec = lax.psum(vec, ("dp", "mp"))
    reps = [vec[i * width : (i + 1) * width] for i in range(6)]
    rest = vec[6 * width :]
    bq = rest[: 3 * nmp * lw].reshape(nmp, 3, lw)
    bu = rest[3 * nmp * lw :].reshape(nmp, -1)
    grad_b_qkv = lax.dynamic_index_in_dim(bq, z, 0, keepdims=False)
    grad_b_up = lax.dynamic_index_in_dim(bu, z, 0, keepdims=False)
    return (
        layer_out,
        grad_inputs,
        reps[0],
        reps[1],
        grad_w_qkv,
        grad_b_qkv,
        grad_w_out,
        reps[2],
        reps[3],
        reps[4],
        grad_w_up,
        grad_b_up,
        grad_w_down,
        reps[5],
    )


def solution(mesh):
    return jax.shard_map(
        body,
        mesh=mesh,
        in_specs=(
            P("dp", "mp", None),
            P("dp"),
            P(),
            P(),
            P(None, None, "mp"),
            P(None, "mp"),
            P("mp", None),
            P(),
            P(),
            P(),
            P(None, "mp"),
            P("mp"),
            P("mp", None),
            P(),
            P("dp", "mp", None),
        ),
        out_specs=(
            P("dp", "mp", None),
            P("dp", "mp", None),
            P(),
            P(),
            P(None, None, "mp"),
            P(None, "mp"),
            P("mp", None),
            P(),
            P(),
            P(),
            P(None, "mp"),
            P("mp"),
            P("mp", None),
            P(),
        ),
        check_vma=False,
    )
```

time: 809 us -> 554 us (0.68)
  waiting for transfers between devices: 491 us -> 114 us
  starting transfers between devices: 0.63 us -> 109 us
  other arithmetic: 83.9 us -> 115 us
  between operations: 15 us -> 3.26 us
  blocking collectives: 56.7 us -> 45.4 us
    all_gather x4 -> x0, waiting for transfers between devices: 238 us -> none  [the longest x1 63.6 us: body(): piece_rows = lax.all_gather(grad_attn, 'mp', axis=1, tiled=True)]
    reduce_scatter x4 -> x0, waiting for transfers between devices: 178 us -> none  [the longest x1 59 us: body(): lax.psum_scatter(attn_terms.astype(jnp.bfloat16), 'mp', scatter_dimension...]
    ppermute x0 -> x85, waiting for transfers between devices: none -> 114 us  [the longest x56 75 us: pair(): return lax.ppermute(x, 'dp', [(i, i ^ 1 << b) for i in range(self.ndp)])]
    ppermute x0 -> x85, starting transfers between devices: none -> 109 us  [the longest x56 46.7 us: pair(): return lax.ppermute(x, 'dp', [(i, i ^ 1 << b) for i in range(self.ndp)])]
    psum x1 -> x0, waiting for transfers between devices: 73.6 us -> none  [body(): lax.psum((grad_w_qkv, grad_b_qkv, grad_w_out, grad_w_up, grad_b_up, grad_...]
    sub x0 -> x1, other arithmetic: none -> 30.8 us  [body(): weights = jnp.exp(scores - row_max)]
    reduce_sum x12 -> x6, other arithmetic: 25.8 us -> 4.68 us  [the longest x1 2.54 us: body(): grad_b_out = jnp.sum(grad_attn, 0, dtype=F32)]
    another operation x4 -> x5, local copies, waits for them, and re-layouts: 11.6 us -> 0.17 us  [the longest x1 0.15 us: body(): jnp.stack([rotate_back(grad_q, cosine, sine_table), rotate_back(grad_k, c...]
  transfers between devices with their start and end apart: 9 -> 85, of which waited for: 9 -> 31; matrix products, arithmetic and copies ran while one was open for 8% -> 40% of each run, Pallas kernels for 0% -> 0%
where the time goes in v1:
time: 554 us; the launch traced here: 546 us
  other arithmetic  115 us (21%)
  waiting for transfers between devices  114 us (21%)
  starting transfers between devices  109 us (20%)
  matrix products  100 us (18%)
  local copies, waits for them, and re-layouts  60.4 us (11%)
  blocking collectives  45.4 us (8%)
    ppermute x56, waiting for transfers between devices, pair(): return lax.ppermute(x, 'dp', [(i, i ^ 1 << b) for i in range(self.ndp)])  75 us
    ppermute x56, starting transfers between devices, pair(): return lax.ppermute(x, 'dp', [(i, i ^ 1 << b) for i in range(self.ndp)])  46.7 us
    psum x1, blocking collectives, body(): vec = lax.psum(vec, ('dp', 'mp'))  45.4 us
    ppermute x21, waiting for transfers between devices, across(): return lax.ppermute(x, 'mp', [(i, i ^ j) for i in range(self.nmp)])  38.6 us
    sub x1, other arithmetic, body(): weights = jnp.exp(scores - row_max)  30.8 us
    ppermute x21, starting transfers between devices, across(): return lax.ppermute(x, 'mp', [(i, i ^ j) for i in range(self.nmp)])  27.1 us
    unnamed x156, local copies, waits for them, and re-layouts  25.8 us
    ppermute x4, starting transfers between devices, to_rows(): out.append(lax.ppermute(mine, ('dp', 'mp'), self.row_perm(k, False)))  23.7 us
  transfers between devices with their start and end apart: 85, of which 31 were waited for; matrix products, arithmetic and copies ran while one was open for 40% of the time, Pallas kernels for 0%

profile of v1, /device:TPU:0, one launch (start us, length us, event | category | flops | bytes accessed | tf_op | source)
XLA Modules:
  0.0 546.3 jit_solution(489637327162286409)
XLA Ops:
  1.7 3.1 collective-permute-start.2
  4.8 2.6 collective-permute-start.3
  17.2 4.0 collective-permute-start.13
  23.9 4.4 collective-permute-start.18
  30.2 2.2 collective-permute-done.4
  34.1 2.8 collective-permute-done.17
  37.1 4.3 collective-permute-done.18
  43.1 17.0 %collective-permute-start.1 = (bf16[256,768]{1,0:T(8,128)(2,1)}, bf16[256,768]{1,0:T(8,128)(2,1)S(1)}, u32[]{:S(2)}, u32[]{:S(2)}) collective-permute-start(bf16[256,768]{1,0:T(8,128)(2,1)} %get-tuple-element.75), channel_id=1, source_target_pairs={{0,1},{1,0},{2,5},{3,4},{4,3},{5,2},{6,7},{7,6},{8,9},{9,8},{10,13... | collective-permute-start | bytes 1179656 | tf_op jit(solution)/shard_map/ppermute | solution.py:94
  64.8 6.2 %collective-permute-done.5 = bf16[3,1,1,1,48,768]{5,4,0,3,2,1:T(8,128)(2,1)S(1)} collective-permute-done((bf16[3,1,1,1,48,768]{5,4,0,3,2,1:T(8,128)(2,1)S(1)}, bf16[3,1,1,1,48,768]{5,4,0,3,2,1:T(8,128)(2,1)S(1)}, u32[]{:S(2)}, u32[]{:S(2)}) %collective-permute-start.5) | collective-permute-done | bytes 221216 | tf_op jit(solution)/shard_map/ppermute | solution.py:75
  72.6 1.9 collective-permute-done.20
  77.8 3.9 collective-permute-done.32
  88.6 6.2 %collective-permute-done.9 = bf16[3,2,1,1,48,768]{5,4,0,1,3,2:T(8,128)(2,1)S(1)} collective-permute-done((bf16[3,2,1,1,48,768]{5,4,0,1,3,2:T(8,128)(2,1)S(1)}, bf16[3,2,1,1,48,768]{5,4,0,1,3,2:T(8,128)(2,1)S(1)}, u32[]{:S(2)}, u32[]{:S(2)}) %collective-permute-start.9) | collective-permute-done | bytes 442400 | tf_op jit(solution)/shard_map/ppermute | solution.py:75
  98.3 7.8 %collective-permute-done.21 = bf16[3,1,2,1,48,768]{5,4,0,3,2,1:T(8,128)(2,1)S(1)} collective-permute-done((bf16[3,1,2,1,48,768]{5,4,0,3,2,1:T(8,128)(2,1)S(1)}, bf16[3,1,2,1,48,768]{5,4,0,3,2,1:T(8,128)(2,1)S(1)}, u32[]{:S(2)}, u32[]{:S(2)}) %collective-permute-start.21) | collective-permute-done | bytes 442400 | tf_op jit(solution)/shard_map/ppermute | solution.py:75
  106.1 4.5 collective-permute-start.37
  118.5 1.8 copy-done.15
  120.4 2.3 bitcast_add_fusion
  131.4 3.1 reverse_select_fusion.2
  137.6 3.1 reverse_select_fusion
  140.6 10.2 %fusion.63 = f32[12,512,1024]{2,1,0:T(8,128)} fusion(bf16[512,12,64]{0,2,1:T(8,128)(2,1)S(1)} %get-tuple-element.29, bf16[512,12,64]{0,2,1:T(8,128)(2,1)S(1)} %collective-permute-done.16, bf16[512,12,64]{0,2,1:T(8,128)(2,1)S(1)} %get-tuple-element.28), kind=kOutput, calls=%fused_computation.173 | convolution fusion | flops 808452096 | bytes 27525120 | tf_op jit(solution)/shard_map/qhe,khe->hqk/dot_general | solution.py:247
  150.8 30.8 %fusion.176 = (f32[12,512]{1,0:T(8,128)S(1)}, f32[12,512,1024]{2,1,0:T(8,128)}) fusion(f32[12,512,1024]{2,1,0:T(8,128)} %fusion.63, pred[1024]{0:T(1024)(128)(4,1)S(1)} %add_compare_fusion), kind=kOutput, calls=%fused_computation.471 | output fusion | flops 37749760 | bytes 50357248 | tf_op jit(solution)/shard_map/sub | solution.py:250
  181.7 14.1 %divide_convert_fusion = bf16[12,512,1024]{2,1,0:T(8,128)(2,1)} fusion(f32[12,512,1024]{2,1,0:T(8,128)} %get-tuple-element.147, f32[12,512]{1,0:T(8,128)S(1)} %get-tuple-element.146), kind=kLoop, calls=%fused_computation.2 | loop fusion | flops 12582912 | bytes 37773312 | tf_op jit(solution)/shard_map/convert_element_type | solution.py:251
  195.8 8.8 %convolution_convert_fusion.4 = bf16[12,64,512]{2,1,0:T(8,128)(2,1)S(1)} fusion(bf16[12,512,1024]{2,1,0:T(8,128)(2,1)} %divide_convert_fusion, bf16[512,12,64]{0,2,1:T(8,128)(2,1)S(1)} %collective-permute-done.14, bf16[512,12,64]{0,2,1:T(8,128)(2,1)S(1)} %fusion.68), kind=kOutput, calls=%fused_computation.149 | convolution fusion | flops 808845312 | bytes 14942208 | tf_op jit(solution)/shard_map/hqk,khe->qhe/dot_general | solution.py:252
  206.0 8.5 %fusion.52 = (u8[512,768]{1,0:T(8,128)(4,1)}, u8[512,768]{1,0:T(8,128)(4,1)}, f32[512,4,768]{2,0,1:T(8,128)S(1)}) fusion(f32[4,768]{1,0:T(4,128)S(1)} %slice.291, bf16[4,768,768]{2,1,0:T(8,128)(2,1)} %bitcast.496, f32[512,768]{1,0:T(8,128)S(1)} %get-tuple-element.149, f32[768]{0:T(1024)S(1)} %copy-done.61, f32[768]{0:T(1024)S(1)} %copy-done.53, ...), kind=kOutput, calls=%fused_computation.143 | convolution fusion | flops 2439118848 | bytes 13391872 | tf_op jit(solution)/shard_map/ld,mdf->lmf/dot_general | solution.py:257
  214.5 6.4 %convert_reduce_fusion = (f32[4,768]{1,0:T(4,128)}, bf16[512,4,768]{2,0,1:T(8,128)(2,1)S(1)}) fusion(f32[512,4,768]{2,0,1:T(8,128)S(1)} %get-tuple-element.150, f32[4,768]{1,0:T(4,128)S(1)} %slice.291, bf16[4,768,768]{2,1,0:T(8,128)(2,1)S(1)} %bitcast.495, f32[512]{0:T(512)S(1)} %copy-done.46, bf16[256,768]{1,0:T(8,128)(2,1)} %collective-permute-done.38, ...), kind=kOutput, calls=%fused_computation.31 | convolution fusion | flops 2438722560 | bytes 14968832 | tf_op jit(solution)/shard_map/ld,mfd->lmf/dot_general | solution.py:267
  221.0 5.0 convolution_convert_fusion.1
  226.1 4.6 fusion.45
  231.8 15.8 %fusion.7 = bf16[512,4,768]{2,0,1:T(8,128)(2,1)S(1)} fusion(f32[512,4,768]{2,0,1:T(8,128)} %copy-done.13, f32[4,768]{1,0:T(4,128)S(1)} %slice.291, u8[512,768]{1,0:T(8,128)(4,1)} %get-tuple-element.15, u8[512,768]{1,0:T(8,128)(4,1)} %get-tuple-element.14), kind=kLoop, calls=%fused_computation.19 | loop fusion | flops 111673344 | bytes 10235904 | tf_op jit(solution)/shard_map/convert_element_type | solution.py:258
  247.7 4.8 convolution_convert_fusion
  260.4 2.5 convert_reduce_fusion.3
  266.5 1.9 copy.182
  268.4 8.5 %convolution_bitcast_fusion = f32[1024,12,64]{0,2,1:T(8,128)} fusion(bf16[512,12,64]{0,2,1:T(8,128)(2,1)S(1)} %bitcast.476, bf16[12,512,1024]{2,1,0:T(8,128)(2,1)} %divide_convert_fusion), kind=kOutput, calls=%fused_computation.77 | convolution fusion | flops 805306368 | bytes 16515072 | tf_op jit(solution)/shard_map/hqk,qhe->khe/dot_general | solution.py:288
  277.7 10.2 %multiply_convert_fusion = bf16[12,512,1024]{2,1,0:T(8,128)(2,1)} fusion(bf16[12,512,1024]{2,1,0:T(8,128)(2,1)} %divide_convert_fusion, f32[12,512]{1,0:T(8,128)} %bitcast.554, bf16[512,12,64]{0,2,1:T(8,128)(2,1)S(1)} %bitcast.477, bf16[512,12,64]{0,2,1:T(8,128)(2,1)} %copy-done.21, bf16[512,12,64]{0,2,1:T(8,128)(2,1)S(1)} %fusion.68), kind=kOutput, calls=%fused_computation.1 | convolution fusion | flops 833617920 | bytes 27549696 | tf_op jit(solution)/shard_map/qhe,khe->hqk/dot_general | solution.py:286
  287.9 7.1 %multiply_bitcast_fusion = f32[1024,12,64]{0,2,1:T(8,128)S(1)} fusion(bf16[512,12,64]{0,2,1:T(8,128)(2,1)S(1)} %copy-done.5, bf16[12,512,1024]{2,1,0:T(8,128)(2,1)} %multiply_convert_fusion), kind=kOutput, calls=%fused_computation.70 | convolution fusion | flops 806092800 | bytes 16515072 | tf_op jit(solution)/shard_map/hqk,qhe->khe/dot_general | solution.py:290
  295.0 8.5 %bitcast_multiply_fusion.1 = (f32[512,12,64]{0,2,1:T(8,128)S(1)}, f32[12,64,512]{2,1,0:T(8,128)S(1)}) fusion(f32[512,64]{0,1:T(8,128)S(1)} %copy-done.38, bf16[12,512,1024]{2,1,0:T(8,128)(2,1)} %multiply_convert_fusion, bf16[512,12,64]{0,2,1:T(8,128)(2,1)S(1)} %copy-done.20, bf16[512,12,64]{0,2,1:T(8,128)(2,1)S(1)} %copy-done.10), kind=kOutput, calls=%fused_computation.123 | convolution fusion | flops 808845312 | bytes 17432576 | tf_op jit(solution)/shard_map/hqk,khe->qhe/dot_general | solution.py:289
  306.2 5.0 fusion.48
  313.1 4.7 collective-permute-start.36
  319.1 2.4 slice.412
  322.1 3.5 convolution_convert_fusion.2
  334.7 2.2 fusion.165
  338.9 3.0 fusion.36
  344.4 2.1 fusion.173
  347.6 4.5 collective-permute-start.42
  364.4 45.4 %psum.7 = f32[9984]{0:T(1024)S(1)} all-reduce(f32[9984]{0:T(1024)S(1)} %constant_dynamic-update-slice_fusion), channel_id=1, replica_groups=mesh['dp'=8,'mp'=4] {'dp','mp'}, use_global_device_ids=true, to_apply=%region_19.20 | all-reduce | flops 9984 | bytes 79872 | tf_op jit(solution)/shard_map/psum | solution.py:329
  414.2 2.3 add_convert_fusion
  416.9 2.3 collective-permute-start.74
  420.8 2.4 add_convert_fusion.1
  425.1 8.3 %collective-permute-done.74 = bf16[4,1,2,1,48,768]{5,4,0,3,2,1:T(8,128)(2,1)S(1)} collective-permute-done((bf16[4,1,2,1,48,768]{5,4,0,3,2,1:T(8,128)(2,1)S(1)}, bf16[4,1,2,1,48,768]{5,4,0,3,2,1:T(8,128)(2,1)S(1)}, u32[]{:S(2)}, u32[]{:S(2)}) %collective-permute-start.74) | collective-permute-done | bytes 589856 | tf_op jit(solution)/shard_map/ppermute | solution.py:75
  433.6 1.9 collective-permute-start.75
  437.3 8.7 %collective-permute-done.60 = bf16[4,1,2,1,48,768]{5,4,0,3,2,1:T(8,128)(2,1)S(1)} collective-permute-done((bf16[4,1,2,1,48,768]{5,4,0,3,2,1:T(8,128)(2,1)S(1)}, bf16[4,1,2,1,48,768]{5,4,0,3,2,1:T(8,128)(2,1)S(1)}, u32[]{:S(2)}, u32[]{:S(2)}) %collective-permute-start.60) | collective-permute-done | bytes 589856 | tf_op jit(solution)/shard_map/ppermute | solution.py:75
  446.2 1.9 collective-permute-start.61
  450.0 2.4 add_convert_fusion.2
  456.2 4.5 collective-permute-done.61
  464.6 8.5 %collective-permute-done.77 = bf16[96,768]{1,0:T(8,128)(2,1)S(1)} collective-permute-done((bf16[96,768]{1,0:T(8,128)(2,1)S(1)}, bf16[96,768]{1,0:T(8,128)(2,1)S(1)}, u32[]{:S(2)}, u32[]{:S(2)}) %collective-permute-start.77) | collective-permute-done | bytes 147488 | tf_op jit(solution)/shard_map/ppermute | solution.py:78
  475.6 9.7 %collective-permute-done.63 = bf16[96,768]{1,0:T(8,128)(2,1)S(1)} collective-permute-done((bf16[96,768]{1,0:T(8,128)(2,1)S(1)}, bf16[96,768]{1,0:T(8,128)(2,1)S(1)}, u32[]{:S(2)}, u32[]{:S(2)}) %collective-permute-start.63) | collective-permute-done | bytes 147488 | tf_op jit(solution)/shard_map/ppermute | solution.py:78
  488.4 1.8 collective-permute-done.82
  490.3 1.9 collective-permute-start.83
  493.4 2.8 collective-permute-done.80
  497.9 3.5 collective-permute-done.69
  505.3 6.2 %collective-permute-done.47 = bf16[4,1,1,1,48,768]{5,4,3,2,1,0:T(8,128)(2,1)S(1)} collective-permute-done((bf16[4,1,1,1,48,768]{5,4,3,2,1,0:T(8,128)(2,1)S(1)}, bf16[4,1,1,1,48,768]{5,4,3,2,1,0:T(8,128)(2,1)S(1)}, u32[]{:S(2)}, u32[]{:S(2)}) %collective-permute-start.47) | collective-permute-done | bytes 294944 | tf_op jit(solution)/shard_map/ppermute | solution.py:75
  512.4 2.2 collective-permute-start.48
  515.0 2.0 collective-permute-start.50
  518.9 8.6 %collective-permute-done.49 = bf16[96,768]{1,0:T(8,128)(2,1)S(1)} collective-permute-done((bf16[96,768]{1,0:T(8,128)(2,1)S(1)}, bf16[96,768]{1,0:T(8,128)(2,1)S(1)}, u32[]{:S(2)}, u32[]{:S(2)}) %collective-permute-start.49) | collective-permute-done | bytes 147488 | tf_op jit(solution)/shard_map/ppermute | solution.py:78
  534.0 2.2 collective-permute-done.54
  538.1 3.4 collective-permute-done.55
  (502 shorter events, 154.0 us)
Async XLA Ops:
  1.7 27.8 %collective-permute-start.2 = (bf16[96,768]{1,0:T(8,128)(2,1)S(1)}, bf16[96,768]{1,0:T(8,128)(2,1)S(1)}, u32[]{:S(2)}, u32[]{:S(2)}) collective-permute-start(bf16[96,768]{1,0:T(8,128)(2,1)S(1)} %fusion.95), channel_id=1, source_target_pairs={{0,1},{1,0},{2,3},{3,2},{4,5},{5,4},{6,7},{7,6},{8,9},{9,8},{10,11... | collective-permute-start | bytes 442376 | tf_op jit(solution)/shard_map/ppermute | solution.py:78
  4.8 24.8 %collective-permute-start.3 = (bf16[96,768]{1,0:T(8,128)(2,1)S(1)}, bf16[96,768]{1,0:T(8,128)(2,1)S(1)}, u32[]{:S(2)}, u32[]{:S(2)}) collective-permute-start(bf16[96,768]{1,0:T(8,128)(2,1)S(1)} %fusion.95), channel_id=1, source_target_pairs={{0,2},{1,3},{2,0},{3,1},{4,6},{5,7},{6,4},{7,5},{8,10},{9,11},{10,... | collective-permute-start | bytes 442376 | tf_op jit(solution)/shard_map/ppermute | solution.py:78
  8.9 14.8 %collective-permute-start.11 = (f32[1344]{0:T(1024)S(1)}, f32[1344]{0:T(1024)S(1)}, u32[]{:S(2)}, u32[]{:S(2)}) collective-permute-start(f32[1344]{0:T(1024)S(1)} %pad_maximum_fusion.30), channel_id=1, source_target_pairs={{0,1},{1,0},{2,3},{3,2},{4,5},{5,4},{6,7},{7,6},{8,9},{9,8},{10,11... | collective-permute-start | bytes 16136 | tf_op jit(solution)/shard_map/ppermute | solution.py:78
  9.4 14.4 %collective-permute-start.12 = (f32[1344]{0:T(1024)S(1)}, f32[1344]{0:T(1024)S(1)}, u32[]{:S(2)}, u32[]{:S(2)}) collective-permute-start(f32[1344]{0:T(1024)S(1)} %pad_maximum_fusion.30), channel_id=1, source_target_pairs={{0,2},{1,3},{2,0},{3,1},{4,6},{5,7},{6,4},{7,5},{8,10},{9,11},{10,... | collective-permute-start | bytes 16136 | tf_op jit(solution)/shard_map/ppermute | solution.py:78
  23.7 8.6 %collective-permute-start.4 = (bf16[96,768]{1,0:T(8,128)(2,1)S(1)}, bf16[96,768]{1,0:T(8,128)(2,1)S(1)}, u32[]{:S(2)}, u32[]{:S(2)}) collective-permute-start(bf16[96,768]{1,0:T(8,128)(2,1)S(1)} %fusion.95), channel_id=1, source_target_pairs={{0,3},{1,2},{2,1},{3,0},{4,7},{5,6},{6,5},{7,4},{8,11},{9,10},{10,... | collective-permute-start | bytes 442376 | tf_op jit(solution)/shard_map/ppermute | solution.py:78
  23.8 13.1 %collective-permute-start.17 = (bf16[96,768]{1,0:T(8,128)(2,1)}, bf16[96,768]{1,0:T(8,128)(2,1)S(1)}, u32[]{:S(2)}, u32[]{:S(2)}) collective-permute-start(bf16[96,768]{1,0:T(8,128)(2,1)} %constant_dynamic-slice_fusion.21), channel_id=1, source_target_pairs={{0,1},{1,0},{2,3},{3,2},{4,5},{5,4},{6,7},{7,6},{8,9},{9,8},{10,11... | collective-permute-start | bytes 442376 | tf_op jit(solution)/shard_map/ppermute | solution.py:78
  23.9 17.5 %collective-permute-start.18 = (bf16[96,768]{1,0:T(8,128)(2,1)}, bf16[96,768]{1,0:T(8,128)(2,1)S(1)}, u32[]{:S(2)}, u32[]{:S(2)}) collective-permute-start(bf16[96,768]{1,0:T(8,128)(2,1)} %constant_dynamic-slice_fusion.21), channel_id=1, source_target_pairs={{0,2},{1,3},{2,0},{3,1},{4,6},{5,7},{6,4},{7,5},{8,10},{9,11},{10,... | collective-permute-start | bytes 442376 | tf_op jit(solution)/shard_map/ppermute | solution.py:78
  29.6 13.5 %collective-permute-start.19 = (bf16[96,768]{1,0:T(8,128)(2,1)}, bf16[96,768]{1,0:T(8,128)(2,1)S(1)}, u32[]{:S(2)}, u32[]{:S(2)}) collective-permute-start(bf16[96,768]{1,0:T(8,128)(2,1)} %constant_dynamic-slice_fusion.21), channel_id=1, source_target_pairs={{0,3},{1,2},{2,1},{3,0},{4,7},{5,6},{6,5},{7,4},{8,11},{9,10},{10,... | collective-permute-start | bytes 442376 | tf_op jit(solution)/shard_map/ppermute | solution.py:78
  29.6 30.6 %collective-permute-start.26 = (bf16[96,768]{1,0:T(8,128)(2,1)S(1)}, bf16[96,768]{1,0:T(8,128)(2,1)S(1)}, u32[]{:S(2)}, u32[]{:S(2)}) collective-permute-start(bf16[96,768]{1,0:T(8,128)(2,1)S(1)} %constant_dynamic-slice_fusion.20), channel_id=1, source_target_pairs={{0,1},{1,0},{2,3},{3,2},{4,5},{5,4},{6,7},{7,6},{8,9},{9,8},{10,11... | collective-permute-start | bytes 442376 | tf_op jit(solution)/shard_map/ppermute | solution.py:78
  32.4 30.3 %collective-permute-start.27 = (bf16[96,768]{1,0:T(8,128)(2,1)S(1)}, bf16[96,768]{1,0:T(8,128)(2,1)S(1)}, u32[]{:S(2)}, u32[]{:S(2)}) collective-permute-start(bf16[96,768]{1,0:T(8,128)(2,1)S(1)} %constant_dynamic-slice_fusion.20), channel_id=1, source_target_pairs={{0,2},{1,3},{2,0},{3,1},{4,6},{5,7},{6,4},{7,5},{8,10},{9,11},{10,... | collective-permute-start | bytes 442376 | tf_op jit(solution)/shard_map/ppermute | solution.py:78
  36.9 27.3 %collective-permute-start.28 = (bf16[96,768]{1,0:T(8,128)(2,1)S(1)}, bf16[96,768]{1,0:T(8,128)(2,1)S(1)}, u32[]{:S(2)}, u32[]{:S(2)}) collective-permute-start(bf16[96,768]{1,0:T(8,128)(2,1)S(1)} %constant_dynamic-slice_fusion.20), channel_id=1, source_target_pairs={{0,3},{1,2},{2,1},{3,0},{4,7},{5,6},{6,5},{7,4},{8,11},{9,10},{10,... | collective-permute-start | bytes 442376 | tf_op jit(solution)/shard_map/ppermute | solution.py:78
  41.4 44.6 %collective-permute-start = (bf16[256,768]{1,0:T(8,128)(2,1)}, bf16[256,768]{1,0:T(8,128)(2,1)S(1)}, u32[]{:S(2)}, u32[]{:S(2)}) collective-permute-start(bf16[256,768]{1,0:T(8,128)(2,1)} %get-tuple-element.74), channel_id=1, source_target_pairs={{0,0},{1,1},{2,4},{3,5},{4,2},{5,3},{6,6},{7,7},{8,8},{9,9},{10,12... | collective-permute-start | bytes 1179656 | tf_op jit(solution)/shard_map/ppermute | solution.py:94
  43.1 43.5 %collective-permute-start.1 = (bf16[256,768]{1,0:T(8,128)(2,1)}, bf16[256,768]{1,0:T(8,128)(2,1)S(1)}, u32[]{:S(2)}, u32[]{:S(2)}) collective-permute-start(bf16[256,768]{1,0:T(8,128)(2,1)} %get-tuple-element.75), channel_id=1, source_target_pairs={{0,1},{1,0},{2,5},{3,4},{4,3},{5,2},{6,7},{7,6},{8,9},{9,8},{10,13... | collective-permute-start | bytes 1179656 | tf_op jit(solution)/shard_map/ppermute | solution.py:94
  60.2 15.9 %collective-permute-start.8 = (bf16[3,1,1,1,48,768]{5,4,0,1,3,2:T(8,128)(2,1)S(1)}, bf16[3,1,1,1,48,768]{5,4,0,1,3,2:T(8,128)(2,1)S(1)}, u32[]{:S(2)}, u32[]{:S(2)}) collective-permute-start(bf16[3,1,1,1,48,768]{5,4,0,1,3,2:T(8,128)(2,1)S(1)} %get-tuple-element.100), channel_id=1, source_target_pairs={{0,16},{4,20},{8,24},{12,28},{16,0},{20,4},{24,8},{28,12},{1,17},{... | collective-permute-start | bytes 663560 | tf_op jit(solution)/shard_map/ppermute | solution.py:75
  62.7 8.3 %collective-permute-start.5 = (bf16[3,1,1,1,48,768]{5,4,0,3,2,1:T(8,128)(2,1)S(1)}, bf16[3,1,1,1,48,768]{5,4,0,3,2,1:T(8,128)(2,1)S(1)}, u32[]{:S(2)}, u32[]{:S(2)}) collective-permute-start(bf16[3,1,1,1,48,768]{5,4,0,3,2,1:T(8,128)(2,1)S(1)} %get-tuple-element.97), channel_id=1, source_target_pairs={{0,8},{4,12},{8,0},{12,4},{16,24},{20,28},{24,16},{28,20},{1,9},{5... | collective-permute-start | bytes 663560 | tf_op jit(solution)/shard_map/ppermute | solution.py:75
  64.2 10.3 %collective-permute-start.20 = (bf16[3,1,1,1,48,768]{5,4,0,3,2,1:T(8,128)(2,1)S(1)}, bf16[3,1,1,1,48,768]{5,4,0,3,2,1:T(8,128)(2,1)S(1)}, u32[]{:S(2)}, u32[]{:S(2)}) collective-permute-start(bf16[3,1,1,1,48,768]{5,4,0,3,2,1:T(8,128)(2,1)S(1)} %get-tuple-element.91), channel_id=1, source_target_pairs={{0,8},{4,12},{8,0},{12,4},{16,24},{20,28},{24,16},{28,20},{1,9},{5... | collective-permute-start | bytes 663560 | tf_op jit(solution)/shard_map/ppermute | solution.py:75
  71.0 12.4 %collective-permute-start.23 = (bf16[3,1,1,1,48,768]{5,4,0,3,2,1:T(8,128)(2,1)S(1)}, bf16[3,1,1,1,48,768]{5,4,0,3,2,1:T(8,128)(2,1)S(1)}, u32[]{:S(2)}, u32[]{:S(2)}) collective-permute-start(bf16[3,1,1,1,48,768]{5,4,0,3,2,1:T(8,128)(2,1)S(1)} %get-tuple-element.94), channel_id=1, source_target_pairs={{0,16},{4,20},{8,24},{12,28},{16,0},{20,4},{24,8},{28,12},{1,17},{... | collective-permute-start | bytes 663560 | tf_op jit(solution)/shard_map/ppermute | solution.py:75
  76.1 9.1 %collective-permute-start.29 = (bf16[3,1,1,1,48,768]{5,4,0,3,2,1:T(8,128)(2,1)S(1)}, bf16[3,1,1,1,48,768]{5,4,0,3,2,1:T(8,128)(2,1)S(1)}, u32[]{:S(2)}, u32[]{:S(2)}) collective-permute-start(bf16[3,1,1,1,48,768]{5,4,0,3,2,1:T(8,128)(2,1)S(1)} %get-tuple-element.90), channel_id=1, source_target_pairs={{0,8},{4,12},{8,0},{12,4},{16,24},{20,28},{24,16},{28,20},{1,9},{5... | collective-permute-start | bytes 663560 | tf_op jit(solution)/shard_map/ppermute | solution.py:75
  81.7 13.1 %collective-permute-start.9 = (bf16[3,2,1,1,48,768]{5,4,0,1,3,2:T(8,128)(2,1)S(1)}, bf16[3,2,1,1,48,768]{5,4,0,1,3,2:T(8,128)(2,1)S(1)}, u32[]{:S(2)}, u32[]{:S(2)}) collective-permute-start(bf16[3,2,1,1,48,768]{5,4,0,1,3,2:T(8,128)(2,1)S(1)} %bitcast_select_fusion), channel_id=1, source_target_pairs={{0,8},{4,12},{8,0},{12,4},{16,24},{20,28},{24,16},{28,20},{1,9},{5... | collective-permute-start | bytes 1327112 | tf_op jit(solution)/shard_map/ppermute | solution.py:75
  83.4 13.2 %collective-permute-start.6 = (bf16[3,1,2,1,48,768]{5,4,0,3,2,1:T(8,128)(2,1)S(1)}, bf16[3,1,2,1,48,768]{5,4,0,3,2,1:T(8,128)(2,1)S(1)}, u32[]{:S(2)}, u32[]{:S(2)}) collective-permute-start(bf16[3,1,2,1,48,768]{5,4,0,3,2,1:T(8,128)(2,1)S(1)} %maximum_select_fusion.16), channel_id=1, source_target_pairs={{0,16},{4,20},{8,24},{12,28},{16,0},{20,4},{24,8},{28,12},{1,17},{... | collective-permute-start | bytes 1327112 | tf_op jit(solution)/shard_map/ppermute | solution.py:75
  85.2 26.5 %collective-permute-start.24 = (bf16[3,2,1,1,48,768]{5,4,0,3,2,1:T(8,128)(2,1)S(1)}, bf16[3,2,1,1,48,768]{5,4,0,3,2,1:T(8,128)(2,1)S(1)}, u32[]{:S(2)}, u32[]{:S(2)}) collective-permute-start(bf16[3,2,1,1,48,768]{5,4,0,3,2,1:T(8,128)(2,1)S(1)} %maximum_select_fusion.21), channel_id=1, source_target_pairs={{0,8},{4,12},{8,0},{12,4},{16,24},{20,28},{24,16},{28,20},{1,9},{5... | collective-permute-start | bytes 1327112 | tf_op jit(solution)/shard_map/ppermute | solution.py:75
  86.0 20.1 %collective-permute-start.21 = (bf16[3,1,2,1,48,768]{5,4,0,3,2,1:T(8,128)(2,1)S(1)}, bf16[3,1,2,1,48,768]{5,4,0,3,2,1:T(8,128)(2,1)S(1)}, u32[]{:S(2)}, u32[]{:S(2)}) collective-permute-start(bf16[3,1,2,1,48,768]{5,4,0,3,2,1:T(8,128)(2,1)S(1)} %maximum_select_fusion.19), channel_id=1, source_target_pairs={{0,16},{4,20},{8,24},{12,28},{16,0},{20,4},{24,8},{28,12},{1,17},{... | collective-permute-start | bytes 1327112 | tf_op jit(solution)/shard_map/ppermute | solution.py:75
  86.6 25.1 %collective-permute-start.33 = (bf16[3,2,1,1,48,768]{5,4,3,2,1,0:T(8,128)(2,1)S(1)}, bf16[3,2,1,1,48,768]{5,4,3,2,1,0:T(8,128)(2,1)S(1)}, u32[]{:S(2)}, u32[]{:S(2)}) collective-permute-start(bf16[3,2,1,1,48,768]{5,4,3,2,1,0:T(8,128)(2,1)S(1)} %copy.175), channel_id=1, source_target_pairs={{0,8},{4,12},{8,0},{12,4},{16,24},{20,28},{24,16},{28,20},{1,9},{5... | collective-permute-start | bytes 1327112 | tf_op jit(solution)/shard_map/ppermute | solution.py:75
  95.0 18.4 %collective-permute-start.10 = (bf16[3,2,2,1,48,768]{5,4,0,1,3,2:T(8,128)(2,1)S(1)}, bf16[3,2,2,1,48,768]{5,4,0,1,3,2:T(8,128)(2,1)S(1)}, u32[]{:S(2)}, u32[]{:S(2)}) collective-permute-start(bf16[3,2,2,1,48,768]{5,4,0,1,3,2:T(8,128)(2,1)S(1)} %maximum_select_fusion.6), channel_id=1, source_target_pairs={{0,4},{4,0},{8,12},{12,8},{16,20},{20,16},{24,28},{28,24},{1,5},{5... | collective-permute-start | bytes 2654216 | tf_op jit(solution)/shard_map/ppermute | solution.py:75
  96.6 16.6 %collective-permute-start.30 = (bf16[3,1,2,1,48,768]{5,4,0,3,2,1:T(8,128)(2,1)S(1)}, bf16[3,1,2,1,48,768]{5,4,0,3,2,1:T(8,128)(2,1)S(1)}, u32[]{:S(2)}, u32[]{:S(2)}) collective-permute-start(bf16[3,1,2,1,48,768]{5,4,0,3,2,1:T(8,128)(2,1)S(1)} %maximum_select_fusion.23), channel_id=1, source_target_pairs={{0,16},{4,20},{8,24},{12,28},{16,0},{20,4},{24,8},{28,12},{1,17},{... | collective-permute-start | bytes 1327112 | tf_op jit(solution)/shard_map/ppermute | solution.py:75
  106.1 108.4 %collective-permute-start.37 = (bf16[256,768]{1,0:T(8,128)(2,1)}, bf16[256,768]{1,0:T(8,128)(2,1)}, u32[]{:S(2)}, u32[]{:S(2)}) collective-permute-start(bf16[256,768]{1,0:T(8,128)(2,1)} %get-tuple-element.68), channel_id=1, source_target_pairs={{0,0},{1,1},{2,4},{3,5},{4,2},{5,3},{6,6},{7,7},{8,8},{9,9},{10,12... | collective-permute-start | bytes 1179656 | tf_op jit(solution)/shard_map/ppermute | solution.py:94
  111.7 102.7 %collective-permute-start.38 = (bf16[256,768]{1,0:T(8,128)(2,1)}, bf16[256,768]{1,0:T(8,128)(2,1)}, u32[]{:S(2)}, u32[]{:S(2)}) collective-permute-start(bf16[256,768]{1,0:T(8,128)(2,1)} %get-tuple-element.69), channel_id=1, source_target_pairs={{0,1},{1,0},{2,5},{3,4},{4,3},{5,2},{6,7},{7,6},{8,9},{9,8},{10,13... | collective-permute-start | bytes 1179656 | tf_op jit(solution)/shard_map/ppermute | solution.py:94
  113.2 11.4 %collective-permute-start.25 = (bf16[3,2,2,1,48,768]{5,4,0,3,2,1:T(8,128)(2,1)S(1)}, bf16[3,2,2,1,48,768]{5,4,0,3,2,1:T(8,128)(2,1)S(1)}, u32[]{:S(2)}, u32[]{:S(2)}) collective-permute-start(bf16[3,2,2,1,48,768]{5,4,0,3,2,1:T(8,128)(2,1)S(1)} %maximum_select_fusion.8), channel_id=1, source_target_pairs={{0,4},{4,0},{8,12},{12,8},{16,20},{20,16},{24,28},{28,24},{1,5},{5... | collective-permute-start | bytes 2654216 | tf_op jit(solution)/shard_map/ppermute | solution.py:75
  113.4 13.8 %collective-permute-start.22 = (bf16[3,2,2,1,48,768]{5,4,0,3,2,1:T(8,128)(2,1)S(1)}, bf16[3,2,2,1,48,768]{5,4,0,3,2,1:T(8,128)(2,1)S(1)}, u32[]{:S(2)}, u32[]{:S(2)}) collective-permute-start(bf16[3,2,2,1,48,768]{5,4,0,3,2,1:T(8,128)(2,1)S(1)} %maximum_select_fusion.7), channel_id=1, source_target_pairs={{0,4},{4,0},{8,12},{12,8},{16,20},{20,16},{24,28},{28,24},{1,5},{5... | collective-permute-start | bytes 2654216 | tf_op jit(solution)/shard_map/ppermute | solution.py:75
  114.4 15.3 %collective-permute-start.34 = (bf16[3,2,2,1,48,768]{5,4,3,2,1,0:T(8,128)(2,1)S(1)}, bf16[3,2,2,1,48,768]{5,4,3,2,1,0:T(8,128)(2,1)S(1)}, u32[]{:S(2)}, u32[]{:S(2)}) collective-permute-start(bf16[3,2,2,1,48,768]{5,4,3,2,1,0:T(8,128)(2,1)S(1)} %maximum_select_fusion.9), channel_id=1, source_target_pairs={{0,4},{4,0},{8,12},{12,8},{16,20},{20,16},{24,28},{28,24},{1,5},{5... | collective-permute-start | bytes 2654216 | tf_op jit(solution)/shard_map/ppermute | solution.py:75
  124.6 9.9 %collective-permute-start.31 = (bf16[3,2,2,1,48,768]{5,4,0,3,2,1:T(8,128)(2,1)S(1)}, bf16[3,2,2,1,48,768]{5,4,0,3,2,1:T(8,128)(2,1)S(1)}, u32[]{:S(2)}, u32[]{:S(2)}) collective-permute-start(bf16[3,2,2,1,48,768]{5,4,0,3,2,1:T(8,128)(2,1)S(1)} %fusion.65), channel_id=1, source_target_pairs={{0,4},{4,0},{8,12},{12,8},{16,20},{20,16},{24,28},{28,24},{1,5},{5... | collective-permute-start | bytes 2654216 | tf_op jit(solution)/shard_map/ppermute | solution.py:75
  127.1 13.5 %collective-permute-start.16 = (bf16[512,12,64]{0,2,1:T(8,128)(2,1)S(1)}, bf16[512,12,64]{0,2,1:T(8,128)(2,1)S(1)}, u32[]{:S(2)}, u32[]{:S(2)}) collective-permute-start(bf16[512,12,64]{0,2,1:T(8,128)(2,1)S(1)} %get-tuple-element.28), channel_id=1, source_target_pairs={{0,4},{4,0},{8,12},{12,8},{16,20},{20,16},{24,28},{28,24},{1,5},{5... | collective-permute-start | bytes 2359304 | tf_op jit(solution)/shard_map/ppermute | solution.py:75
  129.7 66.0 %collective-permute-start.14 = (bf16[512,12,64]{0,2,1:T(8,128)(2,1)S(1)}, bf16[512,12,64]{0,2,1:T(8,128)(2,1)S(1)}, u32[]{:S(2)}, u32[]{:S(2)}) collective-permute-start(bf16[512,12,64]{0,2,1:T(8,128)(2,1)S(1)} %fusion.68), channel_id=1, source_target_pairs={{0,4},{4,0},{8,12},{12,8},{16,20},{20,16},{24,28},{28,24},{1,5},{5... | collective-permute-start | bytes 2359304 | tf_op jit(solution)/shard_map/ppermute | solution.py:75
  255.8 158.4 %collective-permute-start.71 = (bf16[4,2,2,1,96,768]{5,4,0,3,2,1:T(8,128)(2,1)}, bf16[4,2,2,1,96,768]{5,4,0,3,2,1:T(8,128)(2,1)}, u32[]{:S(2)}, u32[]{:S(2)}) collective-permute-start(bf16[4,2,2,1,96,768]{5,4,0,3,2,1:T(8,128)(2,1)} %copy.246), channel_id=1, source_target_pairs={{0,4},{4,0},{8,12},{12,8},{16,20},{20,16},{24,28},{28,24},{1,5},{5... | collective-permute-start | bytes 7077896 | tf_op jit(solution)/shard_map/ppermute | solution.py:75
  259.8 161.0 %collective-permute-start.57 = (bf16[4,2,2,1,96,768]{5,4,0,3,2,1:T(8,128)(2,1)}, bf16[4,2,2,1,96,768]{5,4,0,3,2,1:T(8,128)(2,1)}, u32[]{:S(2)}, u32[]{:S(2)}) collective-permute-start(bf16[4,2,2,1,96,768]{5,4,0,3,2,1:T(8,128)(2,1)} %copy.244), channel_id=1, source_target_pairs={{0,4},{4,0},{8,12},{12,8},{16,20},{20,16},{24,28},{28,24},{1,5},{5... | collective-permute-start | bytes 7077896 | tf_op jit(solution)/shard_map/ppermute | solution.py:75
  304.7 23.1 %collective-permute-start.39 = (bf16[512,12,64]{0,2,1:T(8,128)(2,1)}, bf16[512,12,64]{0,2,1:T(8,128)(2,1)}, u32[]{:S(2)}, u32[]{:S(2)}) collective-permute-start(bf16[512,12,64]{0,2,1:T(8,128)(2,1)} %slice.413), channel_id=1, source_target_pairs={{0,4},{4,0},{8,12},{12,8},{16,20},{20,16},{24,28},{28,24},{1,5},{5... | collective-permute-start | bytes 2359304 | tf_op jit(solution)/shard_map/ppermute | solution.py:75
  312.1 13.5 %collective-permute-start.35 = (bf16[256,768]{1,0:T(8,128)(2,1)}, bf16[256,768]{1,0:T(8,128)(2,1)}, u32[]{:S(2)}, u32[]{:S(2)}) collective-permute-start(bf16[256,768]{1,0:T(8,128)(2,1)} %get-tuple-element.72), channel_id=1, source_target_pairs={{1,0},{0,1},{5,2},{4,3},{3,4},{2,5},{7,6},{6,7},{9,8},{8,9},{13,10... | collective-permute-start | bytes 1179656 | tf_op jit(solution)/shard_map/ppermute | solution.py:99
  313.1 12.6 %collective-permute-start.36 = (bf16[256,768]{1,0:T(8,128)(2,1)}, bf16[256,768]{1,0:T(8,128)(2,1)}, u32[]{:S(2)}, u32[]{:S(2)}) collective-permute-start(bf16[256,768]{1,0:T(8,128)(2,1)} %get-tuple-element.73), channel_id=1, source_target_pairs={{0,0},{1,1},{4,2},{5,3},{2,4},{3,5},{6,6},{7,7},{8,8},{9,9},{12,10... | collective-permute-start | bytes 1179656 | tf_op jit(solution)/shard_map/ppermute | solution.py:99
  346.5 65.3 %collective-permute-start.41 = (bf16[256,768]{1,0:T(8,128)(2,1)}, bf16[256,768]{1,0:T(8,128)(2,1)}, u32[]{:S(2)}, u32[]{:S(2)}) collective-permute-start(bf16[256,768]{1,0:T(8,128)(2,1)} %get-tuple-element.66), channel_id=1, source_target_pairs={{1,0},{0,1},{5,2},{4,3},{3,4},{2,5},{7,6},{6,7},{9,8},{8,9},{13,10... | collective-permute-start | bytes 1179656 | tf_op jit(solution)/shard_map/ppermute | solution.py:99
  347.6 64.2 %collective-permute-start.42 = (bf16[256,768]{1,0:T(8,128)(2,1)}, bf16[256,768]{1,0:T(8,128)(2,1)}, u32[]{:S(2)}, u32[]{:S(2)}) collective-permute-start(bf16[256,768]{1,0:T(8,128)(2,1)} %get-tuple-element.67), channel_id=1, source_target_pairs={{0,0},{1,1},{4,2},{5,3},{2,4},{3,5},{6,6},{7,7},{8,8},{9,9},{12,10... | collective-permute-start | bytes 1179656 | tf_op jit(solution)/shard_map/ppermute | solution.py:99
  409.8 40.2 %collective-permute-start.43 = (bf16[4,2,2,1,96,768]{5,4,3,2,1,0:T(8,128)(2,1)}, bf16[4,2,2,1,96,768]{5,4,3,2,1,0:T(8,128)(2,1)}, u32[]{:S(2)}, u32[]{:S(2)}) collective-permute-start(bf16[4,2,2,1,96,768]{5,4,3,2,1,0:T(8,128)(2,1)} %constant_dynamic-slice_fusion.19), channel_id=1, source_target_pairs={{0,4},{4,0},{8,12},{12,8},{16,20},{20,16},{24,28},{28,24},{1,5},{5... | collective-permute-start | bytes 7077896 | tf_op jit(solution)/shard_map/ppermute | solution.py:75
  416.9 16.5 %collective-permute-start.74 = (bf16[4,1,2,1,48,768]{5,4,0,3,2,1:T(8,128)(2,1)S(1)}, bf16[4,1,2,1,48,768]{5,4,0,3,2,1:T(8,128)(2,1)S(1)}, u32[]{:S(2)}, u32[]{:S(2)}) collective-permute-start(bf16[4,1,2,1,48,768]{5,4,0,3,2,1:T(8,128)(2,1)S(1)} %constant_dynamic-slice_fusion.1), channel_id=1, source_target_pairs={{0,16},{4,20},{8,24},{12,28},{16,0},{20,4},{24,8},{28,12},{1,17},{... | collective-permute-start | bytes 1769480 | tf_op jit(solution)/shard_map/ppermute | solution.py:75
  419.2 16.3 %collective-permute-start.72 = (bf16[4,2,1,1,48,768]{5,4,0,3,2,1:T(8,128)(2,1)S(1)}, bf16[4,2,1,1,48,768]{5,4,0,3,2,1:T(8,128)(2,1)S(1)}, u32[]{:S(2)}, u32[]{:S(2)}) collective-permute-start(bf16[4,2,1,1,48,768]{5,4,0,3,2,1:T(8,128)(2,1)S(1)} %constant_dynamic-slice_fusion.3), channel_id=1, source_target_pairs={{0,8},{4,12},{8,0},{12,4},{16,24},{20,28},{24,16},{28,20},{1,9},{5... | collective-permute-start | bytes 1769480 | tf_op jit(solution)/shard_map/ppermute | solution.py:75
  423.5 22.5 %collective-permute-start.60 = (bf16[4,1,2,1,48,768]{5,4,0,3,2,1:T(8,128)(2,1)S(1)}, bf16[4,1,2,1,48,768]{5,4,0,3,2,1:T(8,128)(2,1)S(1)}, u32[]{:S(2)}, u32[]{:S(2)}) collective-permute-start(bf16[4,1,2,1,48,768]{5,4,0,3,2,1:T(8,128)(2,1)S(1)} %constant_dynamic-slice_fusion.8), channel_id=1, source_target_pairs={{0,16},{4,20},{8,24},{12,28},{16,0},{20,4},{24,8},{28,12},{1,17},{... | collective-permute-start | bytes 1769480 | tf_op jit(solution)/shard_map/ppermute | solution.py:75
  424.0 24.1 %collective-permute-start.58 = (bf16[4,2,1,1,48,768]{5,4,0,3,2,1:T(8,128)(2,1)S(1)}, bf16[4,2,1,1,48,768]{5,4,0,3,2,1:T(8,128)(2,1)S(1)}, u32[]{:S(2)}, u32[]{:S(2)}) collective-permute-start(bf16[4,2,1,1,48,768]{5,4,0,3,2,1:T(8,128)(2,1)S(1)} %constant_dynamic-slice_fusion.10), channel_id=1, source_target_pairs={{0,8},{4,12},{8,0},{12,4},{16,24},{20,28},{24,16},{28,20},{1,9},{5... | collective-permute-start | bytes 1769480 | tf_op jit(solution)/shard_map/ppermute | solution.py:75
  433.6 20.9 %collective-permute-start.75 = (bf16[4,1,1,1,48,768]{5,4,0,3,2,1:T(8,128)(2,1)S(1)}, bf16[4,1,1,1,48,768]{5,4,0,3,2,1:T(8,128)(2,1)S(1)}, u32[]{:S(2)}, u32[]{:S(2)}) collective-permute-start(bf16[4,1,1,1,48,768]{5,4,0,3,2,1:T(8,128)(2,1)S(1)} %constant_dynamic-slice_fusion), channel_id=1, source_target_pairs={{0,8},{4,12},{8,0},{12,4},{16,24},{20,28},{24,16},{28,20},{1,9},{5... | collective-permute-start | bytes 884744 | tf_op jit(solution)/shard_map/ppermute | solution.py:75
  435.7 20.3 %collective-permute-start.73 = (bf16[4,1,1,1,48,768]{5,4,0,3,2,1:T(8,128)(2,1)S(1)}, bf16[4,1,1,1,48,768]{5,4,0,3,2,1:T(8,128)(2,1)S(1)}, u32[]{:S(2)}, u32[]{:S(2)}) collective-permute-start(bf16[4,1,1,1,48,768]{5,4,0,3,2,1:T(8,128)(2,1)S(1)} %constant_dynamic-slice_fusion.2), channel_id=1, source_target_pairs={{0,16},{4,20},{8,24},{12,28},{16,0},{20,4},{24,8},{28,12},{1,17},{... | collective-permute-start | bytes 884744 | tf_op jit(solution)/shard_map/ppermute | solution.py:75
  446.2 14.5 %collective-permute-start.61 = (bf16[4,1,1,1,48,768]{5,4,0,3,2,1:T(8,128)(2,1)S(1)}, bf16[4,1,1,1,48,768]{5,4,0,3,2,1:T(8,128)(2,1)S(1)}, u32[]{:S(2)}, u32[]{:S(2)}) collective-permute-start(bf16[4,1,1,1,48,768]{5,4,0,3,2,1:T(8,128)(2,1)S(1)} %constant_dynamic-slice_fusion.7), channel_id=1, source_target_pairs={{0,8},{4,12},{8,0},{12,4},{16,24},{20,28},{24,16},{28,20},{1,9},{5... | collective-permute-start | bytes 884744 | tf_op jit(solution)/shard_map/ppermute | solution.py:75
  448.4 13.9 %collective-permute-start.59 = (bf16[4,1,1,1,48,768]{5,4,0,3,2,1:T(8,128)(2,1)S(1)}, bf16[4,1,1,1,48,768]{5,4,0,3,2,1:T(8,128)(2,1)S(1)}, u32[]{:S(2)}, u32[]{:S(2)}) collective-permute-start(bf16[4,1,1,1,48,768]{5,4,0,3,2,1:T(8,128)(2,1)S(1)} %constant_dynamic-slice_fusion.9), channel_id=1, source_target_pairs={{0,16},{4,20},{8,24},{12,28},{16,0},{20,4},{24,8},{28,12},{1,17},{... | collective-permute-start | bytes 884744 | tf_op jit(solution)/shard_map/ppermute | solution.py:75
  452.7 48.9 %collective-permute-start.46 = (bf16[4,1,2,1,48,768]{5,4,3,2,1,0:T(8,128)(2,1)S(1)}, bf16[4,1,2,1,48,768]{5,4,3,2,1,0:T(8,128)(2,1)S(1)}, u32[]{:S(2)}, u32[]{:S(2)}) collective-permute-start(bf16[4,1,2,1,48,768]{5,4,3,2,1,0:T(8,128)(2,1)S(1)} %constant_dynamic-slice_fusion.15), channel_id=1, source_target_pairs={{0,16},{4,20},{8,24},{12,28},{16,0},{20,4},{24,8},{28,12},{1,17},{... | collective-permute-start | bytes 1769480 | tf_op jit(solution)/shard_map/ppermute | solution.py:75
  454.4 48.0 %collective-permute-start.44 = (bf16[4,2,1,1,48,768]{5,4,0,3,2,1:T(8,128)(2,1)S(1)}, bf16[4,2,1,1,48,768]{5,4,0,3,2,1:T(8,128)(2,1)S(1)}, u32[]{:S(2)}, u32[]{:S(2)}) collective-permute-start(bf16[4,2,1,1,48,768]{5,4,0,3,2,1:T(8,128)(2,1)S(1)} %copy.242), channel_id=1, source_target_pairs={{0,8},{4,12},{8,0},{12,4},{16,24},{20,28},{24,16},{28,20},{1,9},{5... | collective-permute-start | bytes 1769480 | tf_op jit(solution)/shard_map/ppermute | solution.py:75
  456.2 7.8 %collective-permute-start.76 = (bf16[96,768]{1,0:T(8,128)(2,1)S(1)}, bf16[96,768]{1,0:T(8,128)(2,1)S(1)}, u32[]{:S(2)}, u32[]{:S(2)}) collective-permute-start(bf16[96,768]{1,0:T(8,128)(2,1)S(1)} %get-tuple-element.76), channel_id=1, source_target_pairs={{0,1},{1,0},{2,3},{3,2},{4,5},{5,4},{6,7},{7,6},{8,9},{9,8},{10,11... | collective-permute-start | bytes 442376 | tf_op jit(solution)/shard_map/ppermute | solution.py:78
  460.8 12.4 %collective-permute-start.77 = (bf16[96,768]{1,0:T(8,128)(2,1)S(1)}, bf16[96,768]{1,0:T(8,128)(2,1)S(1)}, u32[]{:S(2)}, u32[]{:S(2)}) collective-permute-start(bf16[96,768]{1,0:T(8,128)(2,1)S(1)} %get-tuple-element.77), channel_id=1, source_target_pairs={{0,2},{1,3},{2,0},{3,1},{4,6},{5,7},{6,4},{7,5},{8,10},{9,11},{10,... | collective-permute-start | bytes 442376 | tf_op jit(solution)/shard_map/ppermute | solution.py:78
  462.2 10.9 %collective-permute-start.78 = (bf16[96,768]{1,0:T(8,128)(2,1)S(1)}, bf16[96,768]{1,0:T(8,128)(2,1)S(1)}, u32[]{:S(2)}, u32[]{:S(2)}) collective-permute-start(bf16[96,768]{1,0:T(8,128)(2,1)S(1)} %get-tuple-element.78), channel_id=1, source_target_pairs={{0,3},{1,2},{2,1},{3,0},{4,7},{5,6},{6,5},{7,4},{8,11},{9,10},{10,... | collective-permute-start | bytes 442376 | tf_op jit(solution)/shard_map/ppermute | solution.py:78
  464.0 10.9 %collective-permute-start.62 = (bf16[96,768]{1,0:T(8,128)(2,1)S(1)}, bf16[96,768]{1,0:T(8,128)(2,1)S(1)}, u32[]{:S(2)}, u32[]{:S(2)}) collective-permute-start(bf16[96,768]{1,0:T(8,128)(2,1)S(1)} %get-tuple-element.79), channel_id=1, source_target_pairs={{0,1},{1,0},{2,3},{3,2},{4,5},{5,4},{6,7},{7,6},{8,9},{9,8},{10,11... | collective-permute-start | bytes 442376 | tf_op jit(solution)/shard_map/ppermute | solution.py:78
  473.2 12.1 %collective-permute-start.63 = (bf16[96,768]{1,0:T(8,128)(2,1)S(1)}, bf16[96,768]{1,0:T(8,128)(2,1)S(1)}, u32[]{:S(2)}, u32[]{:S(2)}) collective-permute-start(bf16[96,768]{1,0:T(8,128)(2,1)S(1)} %get-tuple-element.80), channel_id=1, source_target_pairs={{0,2},{1,3},{2,0},{3,1},{4,6},{5,7},{6,4},{7,5},{8,10},{9,11},{10,... | collective-permute-start | bytes 442376 | tf_op jit(solution)/shard_map/ppermute | solution.py:78
  473.2 12.6 %collective-permute-start.64 = (bf16[96,768]{1,0:T(8,128)(2,1)S(1)}, bf16[96,768]{1,0:T(8,128)(2,1)S(1)}, u32[]{:S(2)}, u32[]{:S(2)}) collective-permute-start(bf16[96,768]{1,0:T(8,128)(2,1)S(1)} %get-tuple-element.81), channel_id=1, source_target_pairs={{0,3},{1,2},{2,1},{3,0},{4,7},{5,6},{6,5},{7,4},{8,11},{9,10},{10,... | collective-permute-start | bytes 442376 | tf_op jit(solution)/shard_map/ppermute | solution.py:78
  474.9 12.5 %collective-permute-start.79 = (bf16[1,1,1,1,48,768]{5,4,3,2,1,0:T(8,128)(2,1)S(1)}, bf16[1,1,1,1,48,768]{5,4,3,2,1,0:T(8,128)(2,1)S(1)}, u32[]{:S(2)}, u32[]{:S(2)}) collective-permute-start(bf16[1,1,1,1,48,768]{5,4,3,2,1,0:T(8,128)(2,1)S(1)} %get-tuple-element.113), channel_id=1, source_target_pairs={{0,8},{4,12},{8,0},{12,4},{16,24},{20,28},{24,16},{28,20},{1,9},{5... | collective-permute-start | bytes 221192 | tf_op jit(solution)/shard_map/ppermute | solution.py:75
  501.4 15.7 %collective-permute-start.67 = (bf16[1,2,2,1,48,768]{5,4,2,3,1,0:T(8,128)(2,1)S(1)}, bf16[1,2,2,1,48,768]{5,4,2,3,1,0:T(8,128)(2,1)S(1)}, u32[]{:S(2)}, u32[]{:S(2)}) collective-permute-start(bf16[1,2,2,1,48,768]{5,4,2,3,1,0:T(8,128)(2,1)S(1)} %maximum_select_fusion.31), channel_id=1, source_target_pairs={{0,4},{4,0},{8,12},{12,8},{16,20},{20,16},{24,28},{28,24},{1,5},{5... | collective-permute-start | bytes 884744 | tf_op jit(solution)/shard_map/ppermute | solution.py:75
  501.7 15.4 %collective-permute-start.70 = (bf16[1,2,2,1,48,768]{5,4,2,3,1,0:T(8,128)(2,1)S(1)}, bf16[1,2,2,1,48,768]{5,4,2,3,1,0:T(8,128)(2,1)S(1)}, u32[]{:S(2)}, u32[]{:S(2)}) collective-permute-start(bf16[1,2,2,1,48,768]{5,4,2,3,1,0:T(8,128)(2,1)S(1)} %copy.215), channel_id=1, source_target_pairs={{0,4},{4,0},{8,12},{12,8},{16,20},{20,16},{24,28},{28,24},{1,5},{5... | collective-permute-start | bytes 884744 | tf_op jit(solution)/shard_map/ppermute | solution.py:75
  502.4 9.0 %collective-permute-start.47 = (bf16[4,1,1,1,48,768]{5,4,3,2,1,0:T(8,128)(2,1)S(1)}, bf16[4,1,1,1,48,768]{5,4,3,2,1,0:T(8,128)(2,1)S(1)}, u32[]{:S(2)}, u32[]{:S(2)}) collective-permute-start(bf16[4,1,1,1,48,768]{5,4,3,2,1,0:T(8,128)(2,1)S(1)} %constant_dynamic-slice_fusion.14), channel_id=1, source_target_pairs={{0,8},{4,12},{8,0},{12,4},{16,24},{20,28},{24,16},{28,20},{1,9},{5... | collective-permute-start | bytes 884744 | tf_op jit(solution)/shard_map/ppermute | solution.py:75
  503.6 8.7 %collective-permute-start.45 = (bf16[4,1,1,1,48,768]{5,4,0,3,2,1:T(8,128)(2,1)S(1)}, bf16[4,1,1,1,48,768]{5,4,0,3,2,1:T(8,128)(2,1)S(1)}, u32[]{:S(2)}, u32[]{:S(2)}) collective-permute-start(bf16[4,1,1,1,48,768]{5,4,0,3,2,1:T(8,128)(2,1)S(1)} %constant_dynamic-slice_fusion.16), channel_id=1, source_target_pairs={{0,16},{4,20},{8,24},{12,28},{16,0},{20,4},{24,8},{28,12},{1,17},{... | collective-permute-start | bytes 884744 | tf_op jit(solution)/shard_map/ppermute | solution.py:75
  514.6 12.9 %collective-permute-start.49 = (bf16[96,768]{1,0:T(8,128)(2,1)S(1)}, bf16[96,768]{1,0:T(8,128)(2,1)S(1)}, u32[]{:S(2)}, u32[]{:S(2)}) collective-permute-start(bf16[96,768]{1,0:T(8,128)(2,1)S(1)} %get-tuple-element.83), channel_id=1, source_target_pairs={{0,2},{1,3},{2,0},{3,1},{4,6},{5,7},{6,4},{7,5},{8,10},{9,11},{10,... | collective-permute-start | bytes 442376 | tf_op jit(solution)/shard_map/ppermute | solution.py:78
  515.0 12.5 %collective-permute-start.50 = (bf16[96,768]{1,0:T(8,128)(2,1)S(1)}, bf16[96,768]{1,0:T(8,128)(2,1)S(1)}, u32[]{:S(2)}, u32[]{:S(2)}) collective-permute-start(bf16[96,768]{1,0:T(8,128)(2,1)S(1)} %get-tuple-element.84), channel_id=1, source_target_pairs={{0,3},{1,2},{2,1},{3,0},{4,7},{5,6},{6,5},{7,4},{8,11},{9,10},{10,... | collective-permute-start | bytes 442376 | tf_op jit(solution)/shard_map/ppermute | solution.py:78
  (94 other events, 939.9 us)
